TPU v7x, 32 devices: a whole 2x2x4 slice. The times are simulated.
32 devices in a mesh: dp: 8 (over z, y), blk: 2 (over core), tensor: 2 (over x).
Axes of the slice: x: 2, y: 2, z: 4, core: 2. Of those that a mesh axis runs over, the one named last changes fastest.
Arguments:
- block_in: bfloat16 [16, 512, 768], P('dp', 'blk'), may hold values from -6 to 6
- crop_shape: int32 [16], P('dp'), may hold values from 0 to 2, as said below
- norm_gains: float32 [2, 768], replicated, may hold values from 0.5 to 1.5
- shifts: float32 [4, 768], replicated, may hold values from -1.75 to 1.75
- qkv_weight: bfloat16 [3, 768, 768], P(None, None, 'tensor'), may hold values from -0.21875 to 0.21875
- qv_bias: float32 [2, 768], P(None, 'tensor'), may hold values from -1.75 to 1.75
- out_weight: bfloat16 [768, 768], P('tensor'), may hold values from -0.875 to 0.875
- up_weight: bfloat16 [768, 3072], P(None, 'tensor'), may hold values from -0.21875 to 0.21875
- up_bias: float32 [3072], P('tensor'), may hold values from -1.75 to 1.75
- down_weight: bfloat16 [3072, 768], P('tensor'), may hold values from -0.109375 to 0.109375
- tconv_weight: bfloat16 [768, 1024], replicated, may hold values from -0.21875 to 0.21875
- kernels: bfloat16 [2, 3456, 128], replicated, may hold values from -0.109375 to 0.109375
- grad_out: bfloat16 [16, 512, 768], P('dp', 'blk'), may hold values from -6 to 6
- grad_decoded: bfloat16 [16, 16, 16, 16, 128], P(('dp', 'tensor'), 'blk'), may hold values from -6 to 6
Outputs:
- block_out: bfloat16 [16, 512, 768], P('dp', 'blk')
- decoded: bfloat16 [16, 16, 16, 16, 128], P(('dp', 'tensor'), 'blk')
- grad_input: bfloat16 [16, 512, 768], P('dp', 'blk')
- grad_gains: float32 [2, 768], replicated
- grad_shifts: float32 [4, 768], replicated
- grad_qkv: float32 [3, 768, 768], P(None, None, 'tensor')
- grad_qv_bias: float32 [2, 768], P(None, 'tensor')
- grad_out_weight: float32 [768, 768], P('tensor')
- grad_up: float32 [768, 3072], P(None, 'tensor')
- grad_up_bias: float32 [3072], P('tensor')
- grad_down: float32 [3072, 768], P('tensor')
- grad_tconv: float32 [768, 1024], P(None, 'tensor')
- grad_kernels: float32 [2, 3456, 128], P(None, None, 'tensor')
Inputs may be any that keep to these rules, and one draw needn't show every extreme that they name: `crop_shape`: among the 2 items held by one index of dp, at least one has id 2.
All inputs are finite; a program needn't handle non-finite values.
Results may differ from a plain program's by a relative error of at most 0.025.
Values may be sent and summed in bfloat16 or wider, within the bound.
A program may use at most 256 MiB of HBM per device.

v0:
```python
import functools
import types

import jax
import jax.numpy as jnp
from jax import lax
from jax.experimental import pallas as pl
from jax.experimental.pallas import tpu as pltpu
from jax.sharding import PartitionSpec as P

HD = 64

MESH = pl.DeviceIdType.MESH
GROUP = 8
FAR = 4


def place():
    dp = lax.axis_index("dp")
    blk = lax.axis_index("blk")
    tensor = lax.axis_index("tensor")
    near = lax.rem(dp, 2)
    far = lax.rem(dp // 2, FAR)
    first = dp // GROUP * GROUP
    return (dp, blk, tensor, near, far, first)


def peers():
    dp, blk, tensor, near, far, first = place()
    core = (dp, 1 - blk, tensor)
    cross = (dp, blk, 1 - tensor)
    beside = (first + 2 * far + 1 - near, blk, tensor)
    side = (first + 2 * (far + 1 - 2 * lax.rem(far, 2)) + near, blk, tensor)
    over = (first + 2 * lax.rem(far + 2, FAR) + near, blk, tensor)
    return (core, cross, beside, side, over)


def greet(devices):
    barrier = pltpu.get_barrier_semaphore()
    for device in devices:
        pl.semaphore_signal(barrier, inc=1, device_id=device, device_id_type=MESH)
    pl.semaphore_wait(barrier, len(devices))


def remote(src, dst, send, recv, device):
    return pltpu.make_async_remote_copy(
        src_ref=src, dst_ref=dst, send_sem=send, recv_sem=recv, device_id=device,
        device_id_type=MESH,
    )


def rows_at(start, size):
    return pl.ds(pl.multiple_of(start, 16), size)


DEPTH = 8
SIDE = 8
WIDE = 16
CH = 128
PAIR = 2 * CH
ROWS = DEPTH * SIDE * WIDE
TAPS = [(deep, wide) for deep in range(3) for wide in range(3)]
PADDED_TAPS = 28


def nt_dot(left, right):
    return lax.dot_general(
        left, right, (((1,), (1,)), ((), ())), preferred_element_type=jnp.float32
    )


def tn_dot(left, right):
    return lax.dot_general(
        left, right, (((0,), (0,)), ((), ())), preferred_element_type=jnp.float32
    )


def dot(left, right):
    return jnp.dot(left, right, preferred_element_type=jnp.float32)


def half_sums(row):
    return row[:, :CH] + row[:, CH:]


def twice(row):
    return jnp.concatenate([row, row], axis=1)


def row_and_column(size):
    return (
        lax.broadcasted_iota(jnp.int32, (size, size), 0),
        lax.broadcasted_iota(jnp.int32, (size, size), 1),
    )


def shift_matrix(step):
    row, column = row_and_column(PAIR)
    same = (row // WIDE) == (column // WIDE)
    return jnp.where(same & (row + step == column), 1.0, 0.0).astype(jnp.bfloat16)


def weave_matrix():
    row, column = row_and_column(PAIR)
    source = lax.rem(row, 2) * CH + row // WIDE * SIDE + lax.rem(row, WIDE) // 2
    return jnp.where(source == column, 1.0, 0.0).astype(jnp.bfloat16)


def unweave_matrix():
    row, column = row_and_column(PAIR)
    source = lax.rem(column, 2) * CH + column // WIDE * SIDE + lax.rem(column, WIDE) // 2
    return jnp.where(source == row, 1.0, 0.0).astype(jnp.bfloat16)


def lay_kernel(kernels_ref, index, weights):
    zero = jnp.zeros((CH, CH), jnp.bfloat16)
    for at, (deep, wide) in enumerate(TAPS):
        weights[at, 3 * CH :, :CH] = zero
        weights[at, :CH, CH:] = zero
        for high in range(3):
            offset = ((deep * 3 + high) * 3 + wide) * CH
            block = kernels_ref[index, offset : offset + CH, :]
            weights[at, high * CH : (high + 1) * CH, :CH] = block
            weights[at, (high + 1) * CH : (high + 2) * CH, CH:] = block


def lay_flipped(kernels_ref, index, weights):
    zero = jnp.zeros((CH, CH), jnp.bfloat16)
    for at, (deep, wide) in enumerate(TAPS):
        weights[at, :CH, 3 * CH :] = zero
        weights[at, CH:, :CH] = zero
        for high in range(3):
            offset = (((2 - deep) * 3 + 2 - high) * 3 + 2 - wide) * CH
            block = kernels_ref[index, offset : offset + CH, :]
            weights[at, :CH, high * CH : (high + 1) * CH] = block
            weights[at, CH:, (high + 1) * CH : (high + 2) * CH] = block


def four_heights(field, wide, start, count):
    depths = pl.ds(start, count)
    low = field[wide, depths, 0:SIDE, :, CH:]
    middle = field[wide, depths, 1 : SIDE + 1, :, :]
    high = field[wide, depths, 2 : SIDE + 2, :, :CH]
    joined = jnp.concatenate([low, middle, high], axis=-1)
    return joined.reshape(count * SIDE * WIDE, 4 * CH)


def conv_tile(field, weights, multiply, level, start):
    total = None
    for at, (deep, wide) in enumerate(TAPS):
        product = multiply(four_heights(field, wide, start + deep, 2), weights[at])
        total = product if total is None else total + product
    level[pl.ds(pl.multiple_of(start * CH, 2 * CH), 2 * CH), :] = total


def conv(field, weights, multiply, level, arrive):
    @pl.loop(0, 2)
    def _(step):
        conv_tile(field, weights, multiply, level, 2 + 2 * step)

    arrive()

    @pl.loop(0, 2)
    def _(step):
        conv_tile(field, weights, multiply, level, 6 * step)


def clear_rims(field, blk):
    for wide in range(3):
        field[wide, :, 0] = jnp.zeros((DEPTH + 2, WIDE, PAIR), jnp.bfloat16)
        field[wide, :, SIDE + 1] = jnp.zeros((DEPTH + 2, WIDE, PAIR), jnp.bfloat16)
        field[wide, 9 * blk] = jnp.zeros((SIDE + 2, WIDE, PAIR), jnp.bfloat16)


def place_rows(field, before, after, step, value):
    shape = (2, SIDE, WIDE, PAIR)
    depths = pl.ds(1 + 2 * step, 2)
    field[1, depths, 1 : SIDE + 1] = value.reshape(shape)
    field[0, depths, 1 : SIDE + 1] = dot(before, value).astype(jnp.bfloat16).reshape(shape)
    field[2, depths, 1 : SIDE + 1] = dot(after, value).astype(jnp.bfloat16).reshape(shape)


def kernel_grad(field, dlevel_turned, index, out, tensor_half):
    for at, (deep, wide) in enumerate(TAPS):
        joined = four_heights(field, wide, deep, DEPTH)
        block = dot(dlevel_turned[...], joined)
        for high in range(3):
            part = (
                block[:CH, high * CH : (high + 1) * CH]
                + block[CH:, (high + 1) * CH : (high + 2) * CH]
            )
            offset = ((deep * 3 + high) * 3 + wide) * CH
            part = part.astype(jnp.bfloat16)
            at = index * PADDED_TAPS * 64 + offset // 2
            for half in range(2):
                out[half, at : at + 64, :] = part[half * 64 : (half + 1) * 64, :]


def decoder_kernel(
    tapped,
    tconv,
    kernels,
    grad_decoded,
    crop_shape,
    decoded,
    block_all,
    dtap_all,
    grad_tconv,
    grad_kernels,
    mask,
    inverse,
    field_one,
    field_two,
    dlevel_two,
    dlevel_one,
    weights_one,
    weights_two,
    flipped_two,
    flipped_one,
    level_one,
    level_two,
    dfield,
    turned_two,
    turned_one,
    dlifted,
    tapped_from,
    dtap_mine,
    dtap_from,
    sums_mine,
    sums_from,
    send,
    recv,
):
    dp, blk, tensor, near, far, first = place()
    core, cross, beside, side, over = peers()
    greet([core, cross])
    low = jnp.bfloat16
    row_tiles = ROWS // PAIR

    copies = []

    def start(index, src, dst, device):
        copy = remote(src, dst, send.at[index], recv.at[index], device)
        copy.start()
        copies.append(copy)
        return copy

    give_tapped = start(0, tapped, tapped_from, cross)

    depth_end, side_end = extents(crop_shape[tensor])
    row = lax.broadcasted_iota(jnp.int32, mask.shape, 0)
    inside = (
        (blk * (DEPTH // 2) + row // (2 * CH) < depth_end)
        & (lax.rem(row // WIDE, SIDE) < side_end)
        & (lax.rem(row, WIDE) // 2 < side_end)
    )
    mask[...] = jnp.where(inside, 1.0, 0.0)
    voxels = (8 * depth_end * side_end * side_end).astype(jnp.float32)
    inverse[...] = 1.0 / jnp.full(inverse.shape, voxels)

    before, after = shift_matrix(-1), shift_matrix(1)

    def send_edge(index, field):
        return start(
            index,
            field.at[:, DEPTH - 7 * blk, 1 : SIDE + 1],
            field.at[:, 9 * blk, 1 : SIDE + 1],
            core,
        )

    def rows_of(step):
        return pl.ds(pl.multiple_of(step * PAIR, PAIR), PAIR)

    def mask_rows(step):
        return twice(mask[rows_of(step), :])

    def totals(slot, pair):
        sums_mine[slot, 0:1, :] = half_sums(pair[0])
        sums_mine[slot, 1:2, :] = half_sums(pair[1])
        return start(5 + slot, sums_mine.at[slot], sums_from.at[slot], core)

    def means(slot, copy):
        copy.wait_recv()
        both = (sums_mine[slot] + sums_from[slot]) * inverse[...]
        return both[0:1, :], both[1:2, :]

    zero_pair = (jnp.zeros((1, PAIR), jnp.float32), jnp.zeros((1, PAIR), jnp.float32))

    for field in (field_one, field_two, dlevel_two, dlevel_one):
        clear_rims(field, blk)
    weave = weave_matrix()
    for piece in range(2):
        tokens = slice(piece * CH, (piece + 1) * CH)
        for a in range(2):
            lifted = dot(tapped[tokens, :], tconv[:, a * 512 : (a + 1) * 512])
            side = [
                jnp.concatenate([lifted[:, c * CH : (c + 1) * CH],
                                 lifted[:, (2 + c) * CH : (3 + c) * CH]], axis=1)
                for c in range(2)
            ]
            woven = dot(weave, jnp.concatenate(side, axis=0).astype(low))
            for depth in range(2):
                at = 2 * (2 * piece + depth) + a
                rows = slice(depth * CH, (depth + 1) * CH)
                value = woven[rows, :] * twice(mask[at * CH : (at + 1) * CH, :])
                level_one[at * CH : (at + 1) * CH, :] = value

    @pl.loop(0, row_tiles)
    def _(step):
        place_rows(field_one, before, after, step, level_one[rows_of(step), :].astype(low))

    edge = send_edge(1, field_one)
    lay_kernel(kernels, 0, weights_one)
    conv(field_one, weights_one, dot, level_one, edge.wait_recv)

    def forward_sums(level):
        def add(step, pair):
            value = level[rows_of(step), :]
            kept = value * mask_rows(step)
            return (
                pair[0] + jnp.sum(kept, axis=0, keepdims=True),
                pair[1] + jnp.sum(kept * value, axis=0, keepdims=True),
            )

        return lax.fori_loop(0, row_tiles, add, zero_pair)

    def mean_and_scale(slot, copy):
        mean, second = means(slot, copy)
        return twice(mean), twice(lax.rsqrt(second - mean * mean + 1e-05))

    def sigmoid(value):
        return 0.5 * jnp.tanh(0.5 * value) + 0.5

    copy = totals(0, forward_sums(level_one))
    lay_kernel(kernels, 1, weights_two)
    mean_one, scale_one = mean_and_scale(0, copy)

    @pl.loop(0, row_tiles)
    def _(step):
        normed = (level_one[rows_of(step), :] - mean_one) * scale_one
        level_one[rows_of(step), :] = normed
        value = normed * sigmoid(normed) * mask_rows(step)
        place_rows(field_two, before, after, step, value.astype(low))

    edge = send_edge(2, field_two)
    lay_flipped(kernels, 1, flipped_two)
    conv(field_two, weights_two, dot, level_two, edge.wait_recv)
    copy = totals(1, forward_sums(level_two))
    lay_flipped(kernels, 0, flipped_one)
    mean_two, scale_two = mean_and_scale(1, copy)

    def two_depths(ref, step, b):
        return ref[pl.ds(2 * step, 2), :, b].reshape(PAIR, CH)

    def decode(step, pair):
        normed = (level_two[rows_of(step), :] - mean_two) * scale_two
        level_two[rows_of(step), :] = normed
        kept = mask_rows(step)
        gate = sigmoid(normed)
        value = (normed * gate * kept).astype(low)
        for b in range(2):
            decoded[pl.ds(2 * step, 2), :, b] = value[:, b * CH : (b + 1) * CH].reshape(
                2, SIDE, WIDE, CH
            )
        grad = jnp.concatenate(
            [two_depths(grad_decoded, step, 0), two_depths(grad_decoded, step, 1)], axis=1
        ).astype(jnp.float32)
        dnormed = gate * (1.0 + normed * (1.0 - gate)) * kept * grad
        dfield[rows_of(step), :] = dnormed
        return (
            pair[0] + jnp.sum(dnormed, axis=0, keepdims=True),
            pair[1] + jnp.sum(dnormed * normed, axis=0, keepdims=True),
        )

    copy = totals(2, lax.fori_loop(0, row_tiles, decode, zero_pair))

    def level_grad(slot, copy, level, scale, field, turned):
        mean_grad, mean_cross = means(slot, copy)
        mean_grad, mean_cross = twice(mean_grad), twice(mean_cross)

        @pl.loop(0, row_tiles)
        def _(step):
            centred = mean_grad + level[rows_of(step), :] * mean_cross
            value = scale * (dfield[rows_of(step), :] - mask_rows(step) * centred)
            place_rows(field, before, after, step, value.astype(low))
            turned[:, rows_of(step)] = value.T.astype(low)

    level_grad(2, copy, level_two, scale_two, dlevel_two, turned_two)
    edge = send_edge(3, dlevel_two)
    conv(dlevel_two, flipped_two, nt_dot, dfield, edge.wait_recv)

    def back_one(step, pair):
        normed = level_one[rows_of(step), :]
        gate = sigmoid(normed)
        dnormed = gate * (1.0 + normed * (1.0 - gate)) * mask_rows(step) * dfield[rows_of(step), :]
        dfield[rows_of(step), :] = dnormed
        return (
            pair[0] + jnp.sum(dnormed, axis=0, keepdims=True),
            pair[1] + jnp.sum(dnormed * normed, axis=0, keepdims=True),
        )

    copy = totals(3, lax.fori_loop(0, row_tiles, back_one, zero_pair))
    level_grad(3, copy, level_one, scale_one, dlevel_one, turned_one)
    edge = send_edge(4, dlevel_one)
    conv(dlevel_one, flipped_one, nt_dot, dfield, edge.wait_recv)

    unweave = unweave_matrix()
    for piece in range(2):
        tokens = slice(piece * CH, (piece + 1) * CH)
        for a in range(2):
            parts = []
            for depth in range(2):
                at = 2 * (2 * piece + depth) + a
                rows = slice(at * CH, (at + 1) * CH)
                parts.append(dfield[rows, :] * twice(mask[rows, :]))
            apart = dot(unweave, jnp.concatenate(parts, axis=0).astype(low)).astype(low)
            for c in range(2):
                for b in range(2):
                    column = ((a * 2 + b) * 2 + c) * CH
                    dlifted[tokens, column : column + CH] = apart[
                        c * CH : (c + 1) * CH, b * CH : (b + 1) * CH
                    ]
    dtap_mine[...] = nt_dot(dlifted[...], tconv[...]).astype(low)
    give_dtap = start(9, dtap_mine, dtap_from, cross)
    for half in range(2):
        lanes = slice(half * 512, (half + 1) * 512)
        grad_tconv[half] = tn_dot(tapped[...], dlifted[:, lanes]).astype(low)
        for index in range(2):
            at = ((index + 1) * PADDED_TAPS - 1) * 64
            grad_kernels[half, at : at + 64, :] = jnp.zeros((64, CH), low)
    kernel_grad(field_two, turned_two, 1, grad_kernels, tensor)
    kernel_grad(field_one, turned_one, 0, grad_kernels, tensor)
    give_tapped.wait_recv()
    block_all[tensor] = tapped[...]
    block_all[1 - tensor] = tapped_from[...]
    give_dtap.wait_recv()
    dtap_all[tensor] = dtap_mine[...]
    dtap_all[1 - tensor] = dtap_from[...]
    for copy in copies:
        copy.wait_send()


def decoder_section(tapped, tconv_weight, kernels, grad_decoded, crop_shape):
    low = jnp.bfloat16
    vmem = pl.BlockSpec(memory_space=pltpu.VMEM)
    field = pltpu.VMEM((3, DEPTH + 2, SIDE + 2, WIDE, PAIR), low)
    plane = pltpu.VMEM((ROWS, PAIR), jnp.float32)
    return pl.pallas_call(
        decoder_kernel,
        out_shape=[
            jax.ShapeDtypeStruct((DEPTH, SIDE, 2, WIDE, CH), low),
            jax.ShapeDtypeStruct((2,) + tapped.shape, low),
            jax.ShapeDtypeStruct((2,) + tapped.shape, low),
            jax.ShapeDtypeStruct((2, tapped.shape[1], tconv_weight.shape[1] // 2), low),
            jax.ShapeDtypeStruct((2, PADDED_TAPS * CH, CH), low),
        ],
        in_specs=[vmem] * 4 + [pl.BlockSpec(memory_space=pltpu.SMEM)],
        out_specs=[vmem] * 5,
        scratch_shapes=[pltpu.VMEM((ROWS, CH), jnp.float32), pltpu.VMEM((8, CH), jnp.float32)]
        + [field] * 4
        + [pltpu.VMEM((9, 4 * CH, PAIR), low)] * 2
        + [pltpu.VMEM((9, PAIR, 4 * CH), low)] * 2
        + [plane] * 3
        + [pltpu.VMEM((PAIR, ROWS), low)] * 2
        + [
            pltpu.VMEM((tapped.shape[0], tconv_weight.shape[1]), low),
            pltpu.VMEM(tapped.shape, low),
            pltpu.VMEM(tapped.shape, low),
            pltpu.VMEM(tapped.shape, low),
            pltpu.VMEM((4, 8, CH), jnp.float32),
            pltpu.VMEM((4, 8, CH), jnp.float32),
            pltpu.SemaphoreType.DMA((10,)),
            pltpu.SemaphoreType.DMA((10,)),
        ],
        name="decoder_section",
        compiler_params=pltpu.CompilerParams(
            collective_id=1, has_side_effects=True, vmem_limit_bytes=60 * 2**20
        ),
    )(tapped, tconv_weight, kernels, grad_decoded, crop_shape)


def widen_rows(src, dst, tile=64):
    @pl.loop(0, src.shape[0] // tile)
    def _(step):
        at = rows_at(step * tile, tile)
        dst[at, :] = src[at, :].astype(jnp.float32)


def finish_kernel(count, *refs):
    sources, refs = refs[:count], refs[count:]
    passed, small, refs = refs[:3], refs[3], refs[4:]
    targets, refs = refs[:count], refs[count:]
    handed, smalls, refs = refs[:3], refs[3:7], refs[7:]
    lows, wides, refs = refs[:count], refs[count : 2 * count], refs[2 * count :]
    held, refs = refs[:3], refs[3:]
    load_sem, store_sem, pass_sem = refs
    loads, stores = [], []
    for index in range(count):
        loads.append(pltpu.make_async_copy(sources[index], lows[index], load_sem.at[index]))
    passes = [
        pltpu.make_async_copy(passed[index], held[index], pass_sem.at[index])
        for index in range(3)
    ]
    for copy in passes + loads:
        copy.start()
    gains, shifts, qv_bias, up_bias = smalls
    width = small.shape[1]
    gains[0:1, :] = small[0:1, :]
    gains[1:2, :] = small[2:3, :]
    shifts[0:1, :] = small[1:2, :]
    shifts[1:4, :] = small[3:6, :]
    qv_bias[0:1, :] = small[6:7, : width // 2]
    qv_bias[1:2, :] = small[6:7, width // 2 :]
    up_bias[:width] = small[7, :]
    up_bias[width:] = small[8, :]

    def store(src, dst):
        copy = pltpu.make_async_copy(src, dst, store_sem.at[len(stores)])
        copy.start()
        stores.append(copy)

    for index in range(3):
        passes[index].wait()
        store(held[index], handed[index])
    for index in range(count):
        src, dst, wide, low = sources[index], targets[index], wides[index], lows[index]
        loads[index].wait()
        if dst.shape == src.shape and len(src.shape) == 2:
            widen_rows(low, wide)
            store(wide, dst)
        elif dst.shape == src.shape:
            for part in range(src.shape[0]):
                widen_rows(low.at[part], wide.at[part])
                store(wide.at[part], dst.at[part])
        elif len(src.shape) == 3:
            for part in range(src.shape[0]):
                widen_rows(low.at[part], wide.at[part])
                columns = src.shape[2]
                store(wide.at[part], dst.at[:, pl.ds(part * columns, columns)])
        elif len(dst.shape) == 2:
            widen_rows(low, wide)
            rows, columns = dst.shape[0], src.shape[1]
            for part in range(2):
                store(
                    wide.at[pl.ds(part * rows, rows)], dst.at[:, pl.ds(part * columns, columns)]
                )
        else:
            kinds, outs, columns = dst.shape
            ins = src.shape[1]
            for kind in range(kinds):
                for tap in range(columns // ins):
                    at = (kind * PADDED_TAPS + tap) * outs
                    wide[kind, :, tap * ins : (tap + 1) * ins] = low[at : at + outs, :].astype(
                        jnp.float32
                    )
                store(wide.at[kind], dst.at[kind])
    for copy in stores:
        copy.wait()


def finish_section(totals, passed, small):
    wide = jnp.float32
    local = totals["qkv"].shape[2]
    width = totals["qkv"].shape[1]
    units = totals["up"].shape[2] * 2
    shapes = {
        "qkv": totals["qkv"].shape,
        "out": (local, width),
        "up": (width, units),
        "down": totals["down"].shape,
        "tconv": totals["tconv"].shape,
        "kernels": (2, 64, 27 * CH),
    }
    count = len(shapes)
    sources = [totals[name] for name in shapes]
    kept = [
        shapes[name] if name == "kernels" else totals[name].shape for name in shapes
    ]
    vmem = pl.BlockSpec(memory_space=pltpu.VMEM)
    hbm = pl.BlockSpec(memory_space=pl.ANY)
    results = pl.pallas_call(
        functools.partial(finish_kernel, count),
        out_shape=[jax.ShapeDtypeStruct(shape, wide) for shape in shapes.values()]
        + [jax.ShapeDtypeStruct(array.shape, array.dtype) for array in passed]
        + [
            jax.ShapeDtypeStruct(shape, wide)
            for shape in ((2, width), (4, width), (2, local), (units,))
        ],
        in_specs=[hbm] * (count + 3) + [vmem],
        out_specs=[hbm] * (count + 3) + [vmem] * 4,
        scratch_shapes=[pltpu.VMEM(array.shape, array.dtype) for array in sources]
        + [pltpu.VMEM(shape, wide) for shape in kept]
        + [pltpu.VMEM(array.shape, array.dtype) for array in passed]
        + [
            pltpu.SemaphoreType.DMA((count,)),
            pltpu.SemaphoreType.DMA((16,)),
            pltpu.SemaphoreType.DMA((3,)),
        ],
        name="finish",
        compiler_params=pltpu.CompilerParams(vmem_limit_bytes=60 * 2**20),
    )(*sources, *passed, small)
    return dict(zip(shapes, results)), results[count : count + 3], results[count + 3 :]


def extents(crop):
    depth = jnp.where(crop == 0, SIDE * 3 // 4, jnp.where(crop == 1, SIDE // 2, SIDE))
    side = jnp.where(crop == 0, SIDE * 3 // 4, SIDE)
    return depth, side


GELU_RATE = 0.7978845608028654
GELU_CUBE = 0.044715


def rows_sum(value):
    return jnp.sum(value, axis=0, keepdims=True)


def lane_mean(value):
    return jnp.mean(value, axis=-1, keepdims=True)


def centred(value):
    centre = value - lane_mean(value)
    return centre, lax.rsqrt(lane_mean(centre * centre) + 1e-06)


def head_only(pair, head):
    lane = lax.broadcasted_iota(jnp.int32, pair.shape, 1)
    return jnp.where((lane // HD) == head, pair, jnp.zeros_like(pair))


def forward_kernel(
    block_in,
    gains,
    shifts,
    qkv_hbm,
    qv_bias,
    out_hbm,
    up_hbm,
    up_bias,
    down_hbm,
    crop_shape,
    normed_one_hbm,
    query_hbm,
    key_value_hbm,
    probs_hbm,
    mixed_hbm,
    middle_hbm,
    normed_two_hbm,
    active_hbm,
    slope_hbm,
    tapped,
    qkv,
    out_weight,
    up,
    down,
    normed_one,
    query,
    key_value,
    probs,
    mixed,
    middle,
    normed_two,
    active,
    slope,
    values_turned,
    part_mine,
    part_from,
    feed_mine,
    feed_from,
    load_sem,
    store_sem,
    send,
    recv,
):
    dp, blk, tensor, near, far, first = place()
    core, cross, beside, side, over = peers()
    low = jnp.bfloat16
    items, slab, width = block_in.shape
    local = query.shape[1]
    units = active.shape[1]

    loads = []
    for index, (src, dst) in enumerate(
        [(qkv_hbm, qkv), (out_hbm, out_weight), (up_hbm, up), (down_hbm, down)]
    ):
        copy = pltpu.make_async_copy(src, dst, load_sem.at[index])
        copy.start()
        loads.append(copy)
    greet([core, cross])
    copies = []
    stores = []

    def start(index, src, dst, device):
        copy = remote(src, dst, send.at[index], recv.at[index], device)
        copy.start()
        copies.append(copy)
        return copy

    def store(src, dst):
        copy = pltpu.make_async_copy(src, dst, store_sem.at[len(stores)])
        copy.start()
        stores.append(copy)

    tile = 64

    for item in range(items):

        @pl.loop(0, slab // tile)
        def _(step):
            value = block_in[item, rows_at(step * tile, tile), :].astype(jnp.float32)
            centre, scale = centred(value)
            normed = centre * scale * gains[0:1, :] + shifts[0:1, :]
            normed_one[rows_at(item * slab + step * tile, tile), :] = normed.astype(low)

    store(normed_one, normed_one_hbm)
    loads[0].wait()
    kv_copies = []
    for item in range(items):
        rows = slice(item * slab, (item + 1) * slab)
        for c in range(2):
            project = dot(normed_one[rows, :], qkv[1 + c])
            if c == 1:
                project = project + qv_bias[1:2, :]
            key_value[item, c, :slab, :] = project.astype(low)
        kv_copies.append(
            start(
                item,
                key_value.at[item, :, pl.ds(0, slab), :],
                key_value.at[item, :, pl.ds(slab, slab), :],
                core,
            )
        )
    for item in range(items):
        rows = slice(item * slab, (item + 1) * slab)
        query[rows, :] = (dot(normed_one[rows, :], qkv[0]) + qv_bias[0:1, :]).astype(low)
    store(query, query_hbm)

    part_copies = []
    for item in range(items):
        rows = slice(item * slab, (item + 1) * slab)
        kv_copies[item].wait_recv()
        values_turned[...] = key_value[item, 1].astype(jnp.float32).T.astype(low)
        depth_end, side_end = extents(crop_shape[item])
        key = lax.broadcasted_iota(jnp.int32, (probs.shape[2], slab), 0)
        patch = jnp.where(key < slab, blk * slab + key, (1 - blk) * slab + key - slab)
        keep = (
            (patch // (SIDE * SIDE) < depth_end)
            & (lax.rem(patch // SIDE, SIDE) < side_end)
            & (lax.rem(patch, SIDE) < side_end)
        )
        for pair in range(local // 128):
            lanes = slice(pair * 128, (pair + 1) * 128)
            keys = key_value[item, 0, :, lanes]
            asked = query[rows, lanes] * jnp.asarray(HD ** (-0.5), low)
            turned = []
            for head in range(2):
                scores = nt_dot(keys, head_only(asked, head))
                scores = jnp.where(keep, scores, -1000000000.0)
                weights = jnp.exp(scores - jnp.max(scores, axis=0, keepdims=True))
                prob = (weights * (1.0 / rows_sum(weights))).astype(low)
                probs[item, 2 * pair + head] = prob
                at = pair * 128 + head * HD
                turned.append(dot(values_turned[at : at + HD, :], prob))
            mixed[rows, lanes] = jnp.concatenate(turned, axis=0).T.astype(low)
        store(probs.at[item], probs_hbm.at[item])
        if item == 0:
            loads[1].wait()
        part_mine[item] = dot(mixed[rows, :], out_weight[...]).astype(low)
        part_copies.append(start(2 + item, part_mine.at[item], part_from.at[item], cross))
    store(key_value, key_value_hbm)
    store(mixed, mixed_hbm)

    for item in range(items):
        if item == 0:
            loads[2].wait()
        part_copies[item].wait_recv()

        @pl.loop(0, slab // tile)
        def _(step):
            at = rows_at(step * tile, tile)
            attended = part_mine[item, at, :].astype(jnp.float32) + part_from[item, at, :].astype(
                jnp.float32
            )
            value = block_in[item, at, :].astype(jnp.float32) + (attended + shifts[2:3, :])
            middle[item, at, :] = value
            centre, scale = centred(value)
            normed = centre * scale * gains[1:2, :] + shifts[1:2, :]
            normed_two[rows_at(item * slab + step * tile, tile), :] = normed.astype(low)

        rows = slice(item * slab, (item + 1) * slab)

        @pl.loop(0, units // 256)
        def _(step):
            lanes = pl.ds(pl.multiple_of(step * 256, 256), 256)
            value = dot(normed_two[rows, :], up[:, lanes]) + up_bias[lanes].reshape(1, -1)
            square = value * value
            bent = jnp.tanh(GELU_RATE * value * (1.0 + GELU_CUBE * square))
            half = 0.5 * (1.0 + bent)
            active[rows, lanes] = (value * half).astype(low)
            inner = GELU_RATE * (1.0 + 3.0 * GELU_CUBE * square)
            slope[rows, lanes] = (half + 0.5 * value * (1.0 - bent * bent) * inner).astype(low)

        if item == 0:
            loads[3].wait()

        @pl.loop(0, width // 256)
        def _(step):
            lanes = pl.ds(pl.multiple_of(step * 256, 256), 256)
            feed_mine[item, :, lanes] = dot(active[rows, :], down[:, lanes]).astype(low)

    store(middle, middle_hbm)
    store(normed_two, normed_two_hbm)
    store(active, active_hbm)
    store(slope, slope_hbm)
    feed = start(4, feed_mine.at[1 - tensor], feed_from, cross)
    feed.wait_recv()

    @pl.loop(0, slab // tile)
    def _(step):
        at = rows_at(step * tile, tile)
        fed = feed_mine[tensor, at, :].astype(jnp.float32) + feed_from[at, :].astype(jnp.float32)
        tapped[at, :] = (middle[tensor, at, :] + (fed + shifts[3:4, :])).astype(low)

    for copy in copies:
        copy.wait_send()
    for copy in stores:
        copy.wait()


def forward_section(
    block_in, gains, shifts, qkv, qv_bias, out_weight, up, up_bias, down, crop_shape
):
    low = jnp.bfloat16
    items, slab, width = block_in.shape
    tokens = items * slab
    local = qkv.shape[2]
    units = up.shape[1]
    heads = local // HD
    patches = 2 * slab
    vmem = pl.BlockSpec(memory_space=pltpu.VMEM)
    hbm = pl.BlockSpec(memory_space=pl.ANY)
    kept = [
        ((tokens, width), low),
        ((tokens, local), low),
        ((items, 2, patches, local), low),
        ((items, heads, patches, slab), low),
        ((tokens, local), low),
        ((items, slab, width), jnp.float32),
        ((tokens, width), low),
        ((tokens, units), low),
        ((tokens, units), low),
    ]
    return pl.pallas_call(
        forward_kernel,
        out_shape=[jax.ShapeDtypeStruct(*one) for one in kept]
        + [jax.ShapeDtypeStruct((slab, width), low)],
        in_specs=[vmem, vmem, vmem, hbm, vmem, hbm, hbm, vmem, hbm]
        + [pl.BlockSpec(memory_space=pltpu.SMEM)],
        out_specs=[hbm] * 9 + [vmem],
        scratch_shapes=[pltpu.VMEM(one.shape, low) for one in (qkv, out_weight, up, down)]
        + [pltpu.VMEM(*one) for one in kept]
        + [
            pltpu.VMEM((local, patches), low),
            pltpu.VMEM(block_in.shape, low),
            pltpu.VMEM(block_in.shape, low),
            pltpu.VMEM(block_in.shape, low),
            pltpu.VMEM((slab, width), low),
            pltpu.SemaphoreType.DMA((4,)),
            pltpu.SemaphoreType.DMA((16,)),
            pltpu.SemaphoreType.DMA((5,)),
            pltpu.SemaphoreType.DMA((5,)),
        ],
        name="forward_section",
        compiler_params=pltpu.CompilerParams(
            collective_id=2, has_side_effects=True, vmem_limit_bytes=60 * 2**20
        ),
    )(block_in, gains, shifts, qkv, qv_bias, out_weight, up, up_bias, down, crop_shape)


def fold(value):
    rows, width = value.shape
    return jnp.sum(value.reshape(rows // 8, 8, width), axis=0)


def add_into(target, target_at, parts, rows, tile):
    @pl.loop(0, rows // tile)
    def _(step):
        at = step * tile
        total = None
        for ref, offset in parts:
            piece = ref[rows_at(offset + at, tile), :].astype(jnp.float32)
            total = piece if total is None else total + piece
        target[rows_at(target_at + at, tile), :] = total.astype(jnp.bfloat16)


COPIES = 10


class Sum:
    def __init__(self, refs, name, index, own, total, full=None):
        self.own, self.total, self.full = own, total, full
        self.from_core = getattr(refs, name + "_core")
        self.from_near = getattr(refs, name + "_near")
        self.from_side = getattr(refs, name + "_side")
        self.from_over = getattr(refs, name + "_over")
        self.part = getattr(refs, name + "_part")
        if full is not None:
            self.both = getattr(refs, name + "_both")
            self.cross_part = getattr(refs, name + "_cross")
        self.send, self.recv = refs.sum_send.at[index], refs.sum_recv.at[index]
        self.local = refs.sum_local.at[index]
        self.rows = total.shape[0]
        self.half, self.quarter = self.rows // 2, self.rows // 4
        self.eighth, self.piece = self.rows // 8, self.rows // 16
        dp, self.blk, self.tensor, self.near, self.far, first = place()
        self.core, self.cross, self.beside, self.side, self.over = peers()
        self.low_bit, self.high_bit = lax.rem(self.far, 2), self.far // 2
        self.near_at = self.blk * self.half + self.near * self.quarter
        self.side_at = self.near_at + self.low_bit * self.eighth
        self.part_at = self.side_at + self.high_bit * self.piece
        self.waiting = []

    def start(self, index, src, dst, device):
        copy = remote(src, dst, self.send.at[index], self.recv.at[index], device)
        copy.start()
        self.waiting.append(copy)
        return copy

    def spread(self, index, at, size, device):
        where = self.total.at[rows_at(at, size)]
        return self.start(index, where, where, device)

    def sA(self):
        give = rows_at((1 - self.blk) * self.half, self.half)
        self.c0 = self.start(0, self.full.at[:, give], self.both, self.core)

    def sB(self):
        self.c0.wait_recv()
        mine = self.blk * self.half
        for which in (1 - self.tensor, self.tensor):
            add_into(
                self.both.at[which], 0, [(self.both.at[which], 0), (self.own.at[which], 0)],
                self.half, self.piece,
            )
        self.cx = self.start(1, self.both.at[1 - self.tensor], self.cross_part, self.cross)

    def s0(self):
        give = rows_at((1 - self.blk) * self.half, self.half)
        self.c0 = self.start(0, self.own.at[give], self.from_core, self.core)

    def s1(self):
        if self.full is None:
            self.c0.wait_recv()
            parts = [(self.from_core, 0), (self.own, self.blk * self.half)]
        else:
            self.cx.wait_recv()
            parts = [(self.both.at[self.tensor], 0), (self.cross_part, 0)]
        add_into(self.from_core, 0, parts, self.half, self.piece)
        give = rows_at((1 - self.near) * self.quarter, self.quarter)
        self.c1 = self.start(2, self.from_core.at[give], self.from_near, self.beside)

    def s2(self):
        self.c1.wait_recv()
        add_into(
            self.from_near, 0, [(self.from_near, 0), (self.from_core, self.near * self.quarter)],
            self.quarter, self.piece,
        )
        give = rows_at((1 - self.low_bit) * self.eighth, self.eighth)
        self.c2 = self.start(3, self.from_near.at[give], self.from_side, self.side)

    def s2b(self):
        self.c2.wait_recv()
        add_into(
            self.from_side, 0, [(self.from_side, 0), (self.from_near, self.low_bit * self.eighth)],
            self.eighth, self.piece,
        )
        give = rows_at((1 - self.high_bit) * self.piece, self.piece)
        self.c2 = self.start(4, self.from_side.at[give], self.from_over, self.over)

    def s3(self):
        self.c2.wait_recv()
        add_into(
            self.part, 0, [(self.from_over, 0), (self.from_side, self.high_bit * self.piece)],
            self.piece, self.piece,
        )
        where = self.total.at[rows_at(self.part_at, self.piece)]
        self.keep = pltpu.make_async_copy(self.part, where, self.local)
        self.keep.start()
        self.c3 = self.start(5, self.part, where, self.over)

    def s3b(self):
        self.keep.wait()
        self.c3.wait_recv()
        self.c3 = self.spread(6, self.side_at, self.eighth, self.side)

    def s4(self):
        self.c3.wait_recv()
        self.c4 = self.spread(7, self.near_at, self.quarter, self.beside)

    def s5(self):
        self.c4.wait_recv()
        self.c5 = self.spread(8, self.blk * self.half, self.half, self.core)

    def s6(self):
        self.c5.wait_recv()
        for copy in self.waiting:
            copy.wait_send()


def sum_scratch(rows, columns):
    low = jnp.bfloat16
    return {
        end: pltpu.VMEM((rows // share, columns), low)
        for end, share in (("_core", 2), ("_near", 4), ("_side", 8), ("_over", 16), ("_part", 16))
    }


def norm_back(value, grad, gain):
    centre, scale = centred(value)
    normed = centre * scale
    scaled = grad * gain
    inner = lane_mean(scaled * normed)
    return scale * (scaled - lane_mean(scaled) - normed * inner), normed


def backward_kernel(layout, *refs):
    r = types.SimpleNamespace(**dict(zip(layout, refs)))
    dp, blk, tensor, near, far, first = place()
    core, cross, beside, side, over = peers()
    low = jnp.bfloat16
    items, slab, width = r.grad_out.shape
    local = r.query.shape[1]
    units = r.active.shape[1]
    pairs = local // 128
    tile = 64
    half_width = width // 2

    loads = {}
    for index, name in enumerate(LOADED):
        copy = pltpu.make_async_copy(getattr(r, name + "_hbm"), getattr(r, name), r.load_sem.at[index])
        copy.start()
        loads[name] = copy
    keep_full = {}
    for index, name in enumerate(("kernels", "tconv")):
        full = getattr(r, "grad_" + name + "_hbm")
        rows = full.shape[1] // 2
        copy = pltpu.make_async_copy(
            full.at[:, rows_at(blk * rows, rows)],
            getattr(r, "own_" + name),
            r.load_sem.at[len(LOADED) + index],
        )
        copy.start()
        keep_full[name] = copy
    greet([core, cross, beside, side, over])
    copies = []

    def start(index, src, dst, device):
        copy = remote(src, dst, r.send.at[index], r.recv.at[index], device)
        copy.start()
        copies.append(copy)
        return copy

    sums = {}
    for h in range(2):
        sums["d%d" % h] = Sum(r, "down%d" % h, h, r.own_down.at[h], r.total_down.at[h])
        sums["u%d" % h] = Sum(r, "up%d" % h, 2 + h, r.own_up.at[h], r.total_up.at[h])
    sums["o"] = Sum(r, "out", 4, r.own_out, r.total_out)
    for c in range(3):
        sums["q%d" % c] = Sum(r, "qkv%d" % c, 5 + c, r.own_qkv.at[c], r.total_qkv.at[c])
    sums["k"] = Sum(r, "kernels", 8, r.own_kernels, r.total_kernels, r.grad_kernels_hbm)
    sums["t"] = Sum(r, "tconv", 9, r.own_tconv, r.total_tconv, r.grad_tconv_hbm)

    def rows_of(item):
        return slice(item * slab, (item + 1) * slab)

    def lanes_of(step, size=256):
        return pl.ds(pl.multiple_of(step * size, size), size)

    r.small[...] = jnp.zeros_like(r.small)

    def dout_rows(item, at):
        return r.grad_out[item, at, :].astype(jnp.float32) + r.dtap[item, at, :].astype(
            jnp.float32
        )

    zero = jnp.zeros((8, width), jnp.float32)

    sent = {}
    waited = set()

    def loaded(*names):
        for name in names:
            if name not in waited:
                loads[name].wait()
                waited.add(name)

    def feed_back(item):
        rows = rows_of(item)

        def shade(step, total):
            value = dout_rows(item, rows_at(step * tile, tile)).astype(low)
            r.ddown[rows_at(item * slab + step * tile, tile), :] = value
            return total + fold(value.astype(jnp.float32))

        total = lax.fori_loop(0, slab // tile, shade, zero)
        r.small[5:6, :] += rows_sum(total)
        loaded("down", "slope")

        @pl.loop(0, units // 256)
        def _(step):
            lanes = lanes_of(step)
            dactive = nt_dot(r.ddown[rows, :], r.down[lanes, :])
            value = (dactive * r.slope[rows, lanes].astype(jnp.float32)).astype(low)
            r.dhidden[rows, lanes] = value
            summed = rows_sum(fold(value.astype(jnp.float32)))
            if item == 0:
                r.bias_sum[0:1, lanes] = summed
            else:
                r.bias_sum[0:1, lanes] += summed

        loaded("up")

        @pl.loop(0, width // 256)
        def _(step):
            value = nt_dot(r.dhidden[rows, :], r.up[lanes_of(step), :])
            r.two_mine[item, :, lanes_of(step)] = value.astype(low)

        sent["dn%d" % item] = start(item, r.two_mine.at[item], r.two_from.at[item], cross)

    def grad_down(h):
        loaded("active")

        @pl.loop(0, units // 2 // 256)
        def _(step):
            lanes = pl.ds(pl.multiple_of(h * (units // 2) + step * 256, 256), 256)
            r.own_down[h, lanes_of(step), :] = tn_dot(r.active[:, lanes], r.ddown[...]).astype(low)

    def grad_up(h):
        loaded("normed_two")

        @pl.loop(0, width // 256)
        def _(step):
            right = r.dhidden[:, h * (units // 2) : (h + 1) * (units // 2)]
            r.own_up[h, lanes_of(step), :] = tn_dot(r.normed_two[:, lanes_of(step)], right).astype(
                low
            )

    def middle_back(item):
        loaded("middle")
        sent["dn%d" % item].wait_recv()

        def back(step, totals):
            at = rows_at(step * tile, tile)
            grad = r.two_mine[item, at, :].astype(jnp.float32) + r.two_from[item, at, :].astype(
                jnp.float32
            )
            dvalue, normed = norm_back(r.middle[item, at, :], grad, r.gains[1:2, :])
            dmiddle = dout_rows(item, at) + dvalue
            r.dmiddle[item, at, :] = dmiddle
            dattn = dmiddle.astype(low)
            r.dattn[rows_at(item * slab + step * tile, tile), :] = dattn
            return (
                totals[0] + fold(grad * normed),
                totals[1] + fold(grad),
                totals[2] + fold(dattn.astype(jnp.float32)),
            )

        totals = lax.fori_loop(0, slab // tile, back, (zero, zero, zero))
        for row, total in zip((2, 3, 4), totals):
            r.small[row : row + 1, :] += rows_sum(total)

    def attention_back(item):
        loaded("out_weight", "key_value", "query", "probs")
        rows = rows_of(item)
        r.keys_turned[...] = r.key_value[item, 0].astype(jnp.float32).T.astype(low)
        r.dmixed[...] = nt_dot(r.dattn[rows, :], r.out_weight[...]).astype(low)
        scale = HD ** (-0.5)
        for pair in range(pairs):
            lanes = slice(pair * 128, (pair + 1) * 128)
            values = r.key_value[item, 1, :, lanes]
            asked = r.query[rows, lanes]
            dmixed = r.dmixed[:, lanes]
            dkeys = dvalues = None
            turned = []
            for head in range(2):
                prob = r.probs[item, 2 * pair + head]
                dmixed_head = head_only(dmixed, head)
                dprob = nt_dot(values, dmixed_head)
                wide = prob.astype(jnp.float32)
                inner = rows_sum(wide * dprob)
                dscores = (wide * (dprob - inner)).astype(low)
                key_part = dot(dscores, head_only(asked, head))
                value_part = dot(prob, dmixed_head)
                dkeys = key_part if dkeys is None else dkeys + key_part
                dvalues = value_part if dvalues is None else dvalues + value_part
                at = pair * 128 + head * HD
                turned.append(dot(r.keys_turned[at : at + HD, :], dscores))
            r.dproject[0, rows, lanes] = (jnp.concatenate(turned, axis=0).T * scale).astype(low)
            dkeys = (dkeys * scale).astype(low)
            dvalues = dvalues.astype(low)
            r.dproject[1, rows, lanes] = dkeys[:slab]
            r.dproject[2, rows, lanes] = dvalues[:slab]
            r.give_kv[item, 0, :, lanes] = dkeys[slab:]
            r.give_kv[item, 1, :, lanes] = dvalues[slab:]
        sent["kv%d" % item] = start(2 + item, r.give_kv.at[item], r.got_kv.at[item], core)

    def grad_out_weight():
        loaded("mixed")
        for h in range(2):
            value = tn_dot(r.mixed[...], r.dattn[:, h * half_width : (h + 1) * half_width])
            r.own_out[h * local : (h + 1) * local, :] = value.astype(low)

    def join_heads():
        for item in range(items):
            sent["kv%d" % item].wait_recv()
            rows = rows_of(item)
            for c in range(2):
                value = r.dproject[1 + c, rows, :].astype(jnp.float32)
                value = value + r.got_kv[item, c].astype(jnp.float32)
                r.dproject[1 + c, rows, :] = value.astype(low)

    def project_back(item):
        loaded("qkv")
        rows = rows_of(item)

        @pl.loop(0, width // 256)
        def _(step):
            lanes = lanes_of(step)
            value = None
            for c in range(3):
                part = nt_dot(r.dproject[c, rows, :], r.qkv[c, lanes, :])
                value = part if value is None else value + part
            r.one_mine[item, :, lanes] = value.astype(low)

        sent["pn%d" % item] = start(4 + item, r.one_mine.at[item], r.one_from.at[item], cross)

    def grad_qkv(c):
        loaded("normed_one")
        r.own_qkv[c] = tn_dot(r.normed_one[...], r.dproject[c]).astype(low)

    def bias_sums():
        for c in (0, 2):
            value = rows_sum(fold(r.dproject[c].astype(jnp.float32)))
            r.small[6:7, (c // 2) * local : (c // 2 + 1) * local] = value
        r.small[7:8, :] = r.bias_sum[0:1, :width]
        r.small[8:9, :] = r.bias_sum[0:1, width:]

    def input_back(item):
        sent["pn%d" % item].wait_recv()

        def back(step, totals):
            at = rows_at(step * tile, tile)
            grad = r.one_mine[item, at, :].astype(jnp.float32) + r.one_from[item, at, :].astype(
                jnp.float32
            )
            value = r.block_in[item, at, :].astype(jnp.float32)
            dvalue, normed = norm_back(value, grad, r.gains[0:1, :])
            r.grad_input[item, at, :] = (r.dmiddle[item, at, :] + dvalue).astype(low)
            return totals[0] + fold(grad * normed), totals[1] + fold(grad)

        totals = lax.fori_loop(0, slab // tile, back, (zero, zero))
        for row, total in zip((0, 1), totals):
            r.small[row : row + 1, :] += rows_sum(total)

    def small_step(index):
        if index > 0:
            sent["small"].wait_recv()
            r.small_sum[index] = r.small_sum[index - 1] + r.small_from[index - 1]
        else:
            r.small_sum[0] = r.small[...]
        if index < 4:
            device = (core, beside, side, over)[index]
            sent["small"] = start(
                6 + index, r.small_sum.at[index], r.small_from.at[index], device
            )
        else:
            r.small_total[...] = r.small_sum[4]

    tasks = {"kv": join_heads, "og": grad_out_weight, "bias": bias_sums}
    for index in range(2):
        for name, work in (
            ("ffn", feed_back),
            ("gd", grad_down),
            ("gu", grad_up),
            ("ln", middle_back),
            ("at", attention_back),
            ("p", project_back),
            ("f", input_back),
        ):
            tasks[name + str(index)] = functools.partial(work, index)
    for c in range(3):
        tasks["gq" + str(c)] = functools.partial(grad_qkv, c)
    for index in range(5):
        tasks["sm" + str(index)] = functools.partial(small_step, index)

    def full_step(name, unit):
        keep_full[{"k": "kernels", "t": "tconv"}[name]].wait()
        unit.sB()

    for name, unit in sums.items():
        for step in ("sA", "sB", "s0", "s1", "s2", "s2b", "s3", "s3b", "s4", "s5", "s6"):
            tasks[name + "." + step] = getattr(unit, step)
        if unit.full is not None:
            tasks[name + ".sB"] = functools.partial(full_step, name, unit)
    for name in ORDER:
        tasks[name]()
    for copy in copies:
        copy.wait_send()


ORDER = (
    "k.sA", "t.sA", "ffn0", "ffn1", "gd1", "d1.s0", "gu1", "u1.s0", "d1.s1", "t.sB", "gd0", "u1.s1",
    "d0.s0", "gu0", "u0.s0", "d0.s1", "ln0", "u0.s1", "at0", "d1.s2", "k.sB", "t.s1", "ln1", "at1",
    "d0.s2", "d1.s2b", "og", "o.s0", "u1.s2", "kv", "p0", "p1", "gq2", "q2.s0", "o.s1", "gq1",
    "q1.s0", "q2.s1", "gq0", "q0.s0", "q1.s1", "d0.s2b", "d1.s3", "u0.s2", "q0.s1", "bias", "u1.s2b", "t.s2",
    "d0.s3", "d1.s3b", "u0.s2b", "u1.s3", "f0", "o.s2", "k.s1", "t.s2b", "d0.s3b", "q2.s2", "d1.s4", "u0.s3",
    "u1.s3b", "q1.s2", "f1", "t.s3", "o.s2b", "q0.s2", "d0.s4", "q2.s2b", "u0.s3b", "sm0", "o.s3", "t.s3b",
    "k.s2", "q1.s2b", "u1.s4", "d1.s5", "q2.s3", "o.s3b", "sm1", "q0.s2b", "q1.s3", "q2.s3b", "k.s2b", "sm2",
    "u0.s4", "q0.s3", "q1.s3b", "d0.s5", "t.s4", "k.s3", "sm3", "q0.s3b", "u1.s5", "o.s4", "d1.s6", "k.s3b",
    "u0.s5", "sm4", "q2.s4", "d0.s6", "t.s5", "q1.s4", "u1.s6", "q0.s4", "o.s5", "u0.s6", "k.s4", "q2.s5",
    "t.s6", "q1.s5", "o.s6", "q0.s5", "q2.s6", "k.s5", "q1.s6", "q0.s6", "k.s6",
)

LOADED = (
    "down",
    "slope",
    "up",
    "active",
    "normed_two",
    "middle",
    "out_weight",
    "key_value",
    "query",
    "probs",
    "mixed",
    "qkv",
    "normed_one",
)


def backward_section(arrays):
    low = jnp.bfloat16
    wide = jnp.float32
    items, slab, width = arrays["grad_out"].shape
    tokens = items * slab
    local = arrays["qkv"].shape[2]
    units = arrays["down"].shape[0]
    patches = arrays["key_value"].shape[2]
    kernel_rows = arrays["grad_kernels"].shape[1]
    near = ["grad_out", "dtap", "block_in", "gains"]
    distant = list(LOADED) + ["grad_kernels", "grad_tconv"]
    totals = {
        "down": (2, units // 2, width),
        "up": (2, width, units // 2),
        "out": (2 * local, width // 2),
        "qkv": (3, width, local),
        "kernels": (kernel_rows, CH),
        "tconv": arrays["grad_tconv"].shape[1:],
    }
    scratch = {name: pltpu.VMEM(arrays[name].shape, arrays[name].dtype) for name in LOADED}
    for name, shape in totals.items():
        full = name in ("kernels", "tconv")
        rows, columns = shape[-2:]
        scratch["own_" + name] = pltpu.VMEM((2, rows // 2, columns) if full else shape, low)
        labels = [name] if len(shape) == 2 else [name + str(part) for part in range(shape[0])]
        for label in labels:
            for end, one in sum_scratch(rows, columns).items():
                scratch[label + end] = one
            if full:
                scratch[label + "_both"] = pltpu.VMEM((2, rows // 2, columns), low)
                scratch[label + "_cross"] = pltpu.VMEM((rows // 2, columns), low)
    block = (items, slab, width)
    for name, shape, dtype in (
        ("ddown", (tokens, width), low),
        ("dhidden", (tokens, units), low),
        ("bias_sum", (8, units), wide),
        ("two_mine", block, low),
        ("two_from", block, low),
        ("dmiddle", block, wide),
        ("dattn", (tokens, width), low),
        ("dmixed", (slab, local), low),
        ("keys_turned", (local, patches), low),
        ("give_kv", (items, 2, slab, local), low),
        ("got_kv", (items, 2, slab, local), low),
        ("dproject", (3, tokens, local), low),
        ("one_mine", block, low),
        ("one_from", block, low),
        ("small", (16, width), wide),
        ("small_sum", (5, 16, width), wide),
        ("small_from", (4, 16, width), wide),
    ):
        scratch[name] = pltpu.VMEM(shape, dtype)
    dma = pltpu.SemaphoreType.DMA
    scratch["load_sem"] = dma((len(LOADED) + 2,))
    scratch["send"] = dma((10,))
    scratch["recv"] = dma((10,))
    scratch["sum_send"] = dma((10, COPIES))
    scratch["sum_recv"] = dma((10, COPIES))
    scratch["sum_local"] = dma((10,))
    outputs = ["grad_input", "small_total"] + ["total_" + name for name in totals]
    layout = near + [name + "_hbm" for name in distant] + outputs + list(scratch)
    vmem = pl.BlockSpec(memory_space=pltpu.VMEM)
    hbm = pl.BlockSpec(memory_space=pl.ANY)
    results = pl.pallas_call(
        functools.partial(backward_kernel, tuple(layout)),
        out_shape=[
            jax.ShapeDtypeStruct(block, low),
            jax.ShapeDtypeStruct((16, width), wide),
        ]
        + [jax.ShapeDtypeStruct(shape, low) for shape in totals.values()],
        in_specs=[vmem] * len(near) + [hbm] * len(distant),
        out_specs=[vmem] * 2 + [hbm] * len(totals),
        scratch_shapes=list(scratch.values()),
        name="backward_section",
        compiler_params=pltpu.CompilerParams(
            collective_id=3, has_side_effects=True, vmem_limit_bytes=62 * 2**20
        ),
    )(*[arrays[name] for name in near + distant])
    return dict(zip(outputs, results))


def body(
    block_in,
    crop_shape,
    norm_gains,
    shifts,
    qkv_weight,
    qv_bias,
    out_weight,
    up_weight,
    up_bias,
    down_weight,
    tconv_weight,
    kernels,
    grad_out,
    grad_decoded,
):
    (
        normed_one,
        query,
        key_value,
        probs,
        mixed,
        middle,
        normed_two,
        active,
        slope,
        tapped,
    ) = forward_section(
        block_in,
        norm_gains,
        shifts,
        qkv_weight,
        qv_bias,
        out_weight,
        up_weight,
        up_bias,
        down_weight,
        crop_shape,
    )
    decoded, block_all, dtap, grad_tconv, grad_kernels = decoder_section(
        tapped,
        tconv_weight,
        kernels,
        grad_decoded.reshape(DEPTH, SIDE, 2, WIDE, CH),
        crop_shape,
    )
    result = backward_section(
        {
            "grad_out": grad_out,
            "dtap": dtap,
            "block_in": block_in,
            "gains": norm_gains,
            "down": down_weight,
            "slope": slope,
            "up": up_weight,
            "active": active,
            "normed_two": normed_two,
            "middle": middle,
            "out_weight": out_weight,
            "key_value": key_value,
            "query": query,
            "probs": probs,
            "mixed": mixed,
            "qkv": qkv_weight,
            "normed_one": normed_one,
            "grad_kernels": grad_kernels,
            "grad_tconv": grad_tconv,
        }
    )
    small = result["small_total"]
    totals = {name[6:]: array for name, array in result.items() if name.startswith("total_")}
    groups = lax.axis_size("dp") // GROUP
    if groups > 1:
        same = [[part * GROUP + i for part in range(groups)] for i in range(GROUP)]
        small = lax.psum(small, "dp", axis_index_groups=same)
        totals = {
            name: lax.psum(array, "dp", axis_index_groups=same) for name, array in totals.items()
        }
    sums, passed, smalls = finish_section(
        totals, (block_all, decoded, result["grad_input"]), small
    )
    return (
        passed[0],
        passed[1].reshape(grad_decoded.shape),
        passed[2],
        smalls[0],
        smalls[1],
        sums["qkv"],
        smalls[2],
        sums["out"],
        sums["up"],
        smalls[3],
        sums["down"].reshape(down_weight.shape),
        sums["tconv"],
        sums["kernels"].transpose(0, 2, 1),
    )


def solution(mesh):
    return jax.shard_map(
        body,
        mesh=mesh,
        in_specs=(
            P("dp", "blk", None),
            P("dp"),
            P(),
            P(),
            P(None, None, "tensor"),
            P(None, "tensor"),
            P("tensor", None),
            P(None, "tensor"),
            P("tensor"),
            P("tensor", None),
            P(),
            P(),
            P("dp", "blk", None),
            P(("dp", "tensor"), "blk", None, None, None),
        ),
        out_specs=(
            P("dp", "blk", None),
            P(("dp", "tensor"), "blk", None, None, None),
            P("dp", "blk", None),
            P(),
            P(),
            P(None, None, "tensor"),
            P(None, "tensor"),
            P("tensor", None),
            P(None, "tensor"),
            P("tensor"),
            P("tensor", None),
            P(None, "tensor"),
            P(None, None, "tensor"),
        ),
        check_vma=False,
    )
```

profile of v0, /device:TPU:0, one launch (start us, length us, event | category | flops | bytes accessed | tf_op | source)
XLA Modules:
  0.0 232.1 jit_solution(3261452362097620378)
XLA Ops:
  0.6 46.4 %forward_section.1 = (bf16[512,768]{1,0:T(8,128)(2,1)}, bf16[512,384]{1,0:T(8,128)(2,1)}, bf16[2,2,512,384]{3,2,1,0:T(8,128)(2,1)}, bf16[2,6,512,256]{3,2,1,0:T(...) custom-call(bf16[2,256,768]{2,1,0:T(8,128)(2,1)} %refs_2_.1, ...), custom_call_target="tpu_custom_call" | custom-call | tf_op jit(solution)/shard_map/forward_section/pallas_call | solution.py:855
  47.1 41.8 %decoder_section.1 = (bf16[8,8,2,16,128]{4,3,2,1,0:T(8,128)(2,1)}, bf16[2,256,768]{2,1,0:T(8,128)(2,1)}, bf16[2,256,768]{2,1,0:T(8,128)(2,1)}, bf16[2,768,512]{2,1,0:T(8,128)(2,1)}, bf16[2,3584,128]{2,1,0:T(8,128)(2,1)}) custom-call(bf16[256,768]{1,0:T(8,128)(2,1)} %get-tuple-element.49.tapped, bf16[768,1024]{1,0:T(8,128)(2,1)} %tconv.1, ...), custom_call_target="tpu_custom_call" | custom-call | tf_op jit(solution)/shard_map/decoder_section/pallas_call | solution.py:448
  88.9 132.0 %backward_section.1 = (bf16[2,256,768]{2,1,0:T(8,128)(2,1)}, f32[16,768]{1,0:T(8,128)}, bf16[2,768,768]{2,1,0:T(8,128)(2,1)}, bf16[2,768,768]{2,1,0:T(8,128)(2,1...) custom-call(bf16[2,256,768]{2,1,0:T(8,128)(2,1)} %refs_0_.1, ...), custom_call_target="tpu_custom_call" | custom-call | tf_op jit(solution)/shard_map/backward_section/pallas_call | solution.py:1406
  220.9 11.0 %finish.1 = (f32[3,768,384]{2,1,0:T(8,128)}, f32[384,768]{1,0:T(8,128)}, f32[768,1536]{1,0:T(8,128)}, f32[2,768,768]{2,1,0:T(8,128)}, f32[768,512]{1,0:T(8,128)}...) custom-call(bf16[3,768,384]{2,1,0:T(8,128)(2,1)} %get-tuple-element., ...), custom_call_target="tpu_custom_call" | custom-call | tf_op jit(solution)/shard_map/finish/pallas_call | solution.py:581
where the time goes:
time: 232 us
  Pallas kernels  231 us (100%)
    pallas_call x1, Pallas kernels, backward_section(): pl.pallas_call(functools.partial(backward_kernel, tuple(layout)), out_sha...  132 us
    pallas_call x1, Pallas kernels, forward_section(): pl.pallas_call(forward_kernel, out_shape=[jax.ShapeDtypeStruct(*one) for...  46.4 us
    pallas_call x1, Pallas kernels, decoder_section(): pl.pallas_call(decoder_kernel, out_shape=[jax.ShapeDtypeStruct((DEPTH, SI...  41.8 us
    pallas_call x1, Pallas kernels, finish_section(): pl.pallas_call(functools.partial(finish_kernel, count), out_shape=[jax.Sh...  11 us

commit v1 on v0

--- a/solution.py
+++ b/solution.py
@@ -716,9 +716,10 @@
 
     store(normed_one, normed_one_hbm)
     loads[0].wait()
+    others = [lax.rem(tensor + step, items) for step in range(items)]
     kv_copies = []
-    for item in range(items):
-        rows = slice(item * slab, (item + 1) * slab)
+    for place_at, item in enumerate(others):
+        rows = rows_at(item * slab, slab)
         for c in range(2):
             project = dot(normed_one[rows, :], qkv[1 + c])
             if c == 1:
@@ -726,21 +727,21 @@
             key_value[item, c, :slab, :] = project.astype(low)
         kv_copies.append(
             start(
-                item,
+                place_at,
                 key_value.at[item, :, pl.ds(0, slab), :],
                 key_value.at[item, :, pl.ds(slab, slab), :],
                 core,
             )
         )
-    for item in range(items):
-        rows = slice(item * slab, (item + 1) * slab)
+    for item in others:
+        rows = rows_at(item * slab, slab)
         query[rows, :] = (dot(normed_one[rows, :], qkv[0]) + qv_bias[0:1, :]).astype(low)
     store(query, query_hbm)
 
     part_copies = []
-    for item in range(items):
-        rows = slice(item * slab, (item + 1) * slab)
-        kv_copies[item].wait_recv()
+    for place_at, item in enumerate(others):
+        rows = rows_at(item * slab, slab)
+        kv_copies[place_at].wait_recv()
         values_turned[...] = key_value[item, 1].astype(jnp.float32).T.astype(low)
         depth_end, side_end = extents(crop_shape[item])
         key = lax.broadcasted_iota(jnp.int32, (probs.shape[2], slab), 0)
@@ -765,17 +766,17 @@
                 turned.append(dot(values_turned[at : at + HD, :], prob))
             mixed[rows, lanes] = jnp.concatenate(turned, axis=0).T.astype(low)
         store(probs.at[item], probs_hbm.at[item])
-        if item == 0:
+        if place_at == 0:
             loads[1].wait()
         part_mine[item] = dot(mixed[rows, :], out_weight[...]).astype(low)
-        part_copies.append(start(2 + item, part_mine.at[item], part_from.at[item], cross))
+        part_copies.append(start(2 + place_at, part_mine.at[item], part_from.at[item], cross))
     store(key_value, key_value_hbm)
     store(mixed, mixed_hbm)
 
-    for item in range(items):
-        if item == 0:
+    for place_at, item in enumerate(others[1:] + others[:1]):
+        if place_at == 0:
             loads[2].wait()
-        part_copies[item].wait_recv()
+        part_copies[place_at].wait_recv()
 
         @pl.loop(0, slab // tile)
         def _(step):
@@ -789,7 +790,7 @@
             normed = centre * scale * gains[1:2, :] + shifts[1:2, :]
             normed_two[rows_at(item * slab + step * tile, tile), :] = normed.astype(low)
 
-        rows = slice(item * slab, (item + 1) * slab)
+        rows = rows_at(item * slab, slab)
 
         @pl.loop(0, units // 256)
         def _(step):
@@ -802,7 +803,7 @@
             inner = GELU_RATE * (1.0 + 3.0 * GELU_CUBE * square)
             slope[rows, lanes] = (half + 0.5 * value * (1.0 - bent * bent) * inner).astype(low)
 
-        if item == 0:
+        if place_at == 0:
             loads[3].wait()
 
         @pl.loop(0, width // 256)
@@ -810,11 +811,13 @@
             lanes = pl.ds(pl.multiple_of(step * 256, 256), 256)
             feed_mine[item, :, lanes] = dot(active[rows, :], down[:, lanes]).astype(low)
 
+        if place_at == 0:
+            feed = start(4, feed_mine.at[item], feed_from, cross)
+
     store(middle, middle_hbm)
     store(normed_two, normed_two_hbm)
     store(active, active_hbm)
     store(slope, slope_hbm)
-    feed = start(4, feed_mine.at[1 - tensor], feed_from, cross)
     feed.wait_recv()
 
     @pl.loop(0, slab // tile)
@@ -899,122 +902,111 @@
 
 
 class Sum:
-    def __init__(self, refs, name, index, own, total, full=None):
+    def __init__(self, refs, name, index, path, own, total, full=None):
         self.own, self.total, self.full = own, total, full
-        self.from_core = getattr(refs, name + "_core")
-        self.from_near = getattr(refs, name + "_near")
-        self.from_side = getattr(refs, name + "_side")
-        self.from_over = getattr(refs, name + "_over")
+        self.held = [getattr(refs, name + end) for end in ("_core", "_first", "_second", "_third")]
         self.part = getattr(refs, name + "_part")
         if full is not None:
             self.both = getattr(refs, name + "_both")
             self.cross_part = getattr(refs, name + "_cross")
         self.send, self.recv = refs.sum_send.at[index], refs.sum_recv.at[index]
         self.local = refs.sum_local.at[index]
-        self.rows = total.shape[0]
-        self.half, self.quarter = self.rows // 2, self.rows // 4
-        self.eighth, self.piece = self.rows // 8, self.rows // 16
-        dp, self.blk, self.tensor, self.near, self.far, first = place()
-        self.core, self.cross, self.beside, self.side, self.over = peers()
-        self.low_bit, self.high_bit = lax.rem(self.far, 2), self.far // 2
-        self.near_at = self.blk * self.half + self.near * self.quarter
-        self.side_at = self.near_at + self.low_bit * self.eighth
-        self.part_at = self.side_at + self.high_bit * self.piece
+        rows = total.shape[0]
+        self.half, self.piece = rows // 2, rows // 16
+        dp, self.blk, self.tensor, near, far, first = place()
+        self.core, self.cross, beside, side, over = peers()
+        self.stages = [
+            {"y": (beside, near), "s": (side, lax.rem(far, 2)), "o": (over, far // 2)}[one]
+            for one in path
+        ]
+        self.at = [self.blk * self.half]
+        for stage, (device, bit) in enumerate(self.stages):
+            self.at.append(self.at[-1] + bit * (rows >> (stage + 2)))
+        self.sizes = [rows >> (stage + 1) for stage in range(4)]
         self.waiting = []
 
     def start(self, index, src, dst, device):
         copy = remote(src, dst, self.send.at[index], self.recv.at[index], device)
         copy.start()
         self.waiting.append(copy)
-        return copy
-
-    def spread(self, index, at, size, device):
-        where = self.total.at[rows_at(at, size)]
-        return self.start(index, where, where, device)
+        self.last = copy
 
     def sA(self):
         give = rows_at((1 - self.blk) * self.half, self.half)
-        self.c0 = self.start(0, self.full.at[:, give], self.both, self.core)
+        self.start(0, self.full.at[:, give], self.both, self.core)
 
     def sB(self):
-        self.c0.wait_recv()
-        mine = self.blk * self.half
+        self.last.wait_recv()
         for which in (1 - self.tensor, self.tensor):
             add_into(
                 self.both.at[which], 0, [(self.both.at[which], 0), (self.own.at[which], 0)],
                 self.half, self.piece,
             )
-        self.cx = self.start(1, self.both.at[1 - self.tensor], self.cross_part, self.cross)
+        self.start(1, self.both.at[1 - self.tensor], self.cross_part, self.cross)
 
     def s0(self):
         give = rows_at((1 - self.blk) * self.half, self.half)
-        self.c0 = self.start(0, self.own.at[give], self.from_core, self.core)
+        self.start(0, self.own.at[give], self.held[0], self.core)
+
+    def narrow(self, stage):
+        device, bit = self.stages[stage]
+        give = rows_at((1 - bit) * self.sizes[stage + 1], self.sizes[stage + 1])
+        self.start(2 + stage, self.held[stage].at[give], self.held[stage + 1], device)
+
+    def gather(self, stage, target):
+        self.last.wait_recv()
+        size = self.sizes[stage]
+        kept = (self.held[stage - 1], self.stages[stage - 1][1] * size)
+        add_into(target, 0, [(self.held[stage], 0), kept], size, self.piece)
 
     def s1(self):
-        if self.full is None:
-            self.c0.wait_recv()
-            parts = [(self.from_core, 0), (self.own, self.blk * self.half)]
-        else:
-            self.cx.wait_recv()
+        self.last.wait_recv()
+        parts = [(self.held[0], 0), (self.own, self.blk * self.half)]
+        if self.full is not None:
             parts = [(self.both.at[self.tensor], 0), (self.cross_part, 0)]
-        add_into(self.from_core, 0, parts, self.half, self.piece)
-        give = rows_at((1 - self.near) * self.quarter, self.quarter)
-        self.c1 = self.start(2, self.from_core.at[give], self.from_near, self.beside)
+        add_into(self.held[0], 0, parts, self.half, self.piece)
+        self.narrow(0)
 
     def s2(self):
-        self.c1.wait_recv()
-        add_into(
-            self.from_near, 0, [(self.from_near, 0), (self.from_core, self.near * self.quarter)],
-            self.quarter, self.piece,
-        )
-        give = rows_at((1 - self.low_bit) * self.eighth, self.eighth)
-        self.c2 = self.start(3, self.from_near.at[give], self.from_side, self.side)
+        self.gather(1, self.held[1])
+        self.narrow(1)
 
     def s2b(self):
-        self.c2.wait_recv()
-        add_into(
-            self.from_side, 0, [(self.from_side, 0), (self.from_near, self.low_bit * self.eighth)],
-            self.eighth, self.piece,
-        )
-        give = rows_at((1 - self.high_bit) * self.piece, self.piece)
-        self.c2 = self.start(4, self.from_side.at[give], self.from_over, self.over)
+        self.gather(2, self.held[2])
+        self.narrow(2)
 
     def s3(self):
-        self.c2.wait_recv()
-        add_into(
-            self.part, 0, [(self.from_over, 0), (self.from_side, self.high_bit * self.piece)],
-            self.piece, self.piece,
-        )
-        where = self.total.at[rows_at(self.part_at, self.piece)]
+        self.gather(3, self.part)
+        where = self.total.at[rows_at(self.at[3], self.piece)]
         self.keep = pltpu.make_async_copy(self.part, where, self.local)
         self.keep.start()
-        self.c3 = self.start(5, self.part, where, self.over)
+        self.start(5, self.part, where, self.stages[2][0])
+
+    def spread(self, index, at, size, device):
+        self.last.wait_recv()
+        where = self.total.at[rows_at(at, size)]
+        self.start(index, where, where, device)
 
     def s3b(self):
         self.keep.wait()
-        self.c3.wait_recv()
-        self.c3 = self.spread(6, self.side_at, self.eighth, self.side)
+        self.spread(6, self.at[2], self.sizes[2], self.stages[1][0])
 
     def s4(self):
-        self.c3.wait_recv()
-        self.c4 = self.spread(7, self.near_at, self.quarter, self.beside)
+        self.spread(7, self.at[1], self.sizes[1], self.stages[0][0])
 
     def s5(self):
-        self.c4.wait_recv()
-        self.c5 = self.spread(8, self.blk * self.half, self.half, self.core)
+        self.spread(8, self.at[0], self.sizes[0], self.core)
 
     def s6(self):
-        self.c5.wait_recv()
+        self.last.wait_recv()
         for copy in self.waiting:
             copy.wait_send()
 
 
 def sum_scratch(rows, columns):
     low = jnp.bfloat16
-    return {
-        end: pltpu.VMEM((rows // share, columns), low)
-        for end, share in (("_core", 2), ("_near", 4), ("_side", 8), ("_over", 16), ("_part", 16))
-    }
+    shares = {"_core": 2, "_first": 4, "_second": 8, "_third": 16, "_part": 16}
+    return {end: pltpu.VMEM((rows // share, columns), low) for end, share in shares.items()}
 
 
 def norm_back(value, grad, gain):
@@ -1064,13 +1056,17 @@
 
     sums = {}
     for h in range(2):
-        sums["d%d" % h] = Sum(r, "down%d" % h, h, r.own_down.at[h], r.total_down.at[h])
-        sums["u%d" % h] = Sum(r, "up%d" % h, 2 + h, r.own_up.at[h], r.total_up.at[h])
-    sums["o"] = Sum(r, "out", 4, r.own_out, r.total_out)
+        sums["d%d" % h] = ("down%d" % h, r.own_down.at[h], r.total_down.at[h])
+        sums["u%d" % h] = ("up%d" % h, r.own_up.at[h], r.total_up.at[h])
+    sums["o"] = ("out", r.own_out, r.total_out)
     for c in range(3):
-        sums["q%d" % c] = Sum(r, "qkv%d" % c, 5 + c, r.own_qkv.at[c], r.total_qkv.at[c])
-    sums["k"] = Sum(r, "kernels", 8, r.own_kernels, r.total_kernels, r.grad_kernels_hbm)
-    sums["t"] = Sum(r, "tconv", 9, r.own_tconv, r.total_tconv, r.grad_tconv_hbm)
+        sums["q%d" % c] = ("qkv%d" % c, r.own_qkv.at[c], r.total_qkv.at[c])
+    sums["k"] = ("kernels", r.own_kernels, r.total_kernels, r.grad_kernels_hbm)
+    sums["t"] = ("tconv", r.own_tconv, r.total_tconv, r.grad_tconv_hbm)
+    sums = {
+        name: Sum(r, one[0], index, PATHS[name], *one[1:])
+        for index, (name, one) in enumerate(sums.items())
+    }
 
     def rows_of(item):
         return slice(item * slab, (item + 1) * slab)
@@ -1096,9 +1092,7 @@
                 loads[name].wait()
                 waited.add(name)
 
-    def feed_back(item):
-        rows = rows_of(item)
-
+    def shade_rows(item):
         def shade(step, total):
             value = dout_rows(item, rows_at(step * tile, tile)).astype(low)
             r.ddown[rows_at(item * slab + step * tile, tile), :] = value
@@ -1106,6 +1100,9 @@
 
         total = lax.fori_loop(0, slab // tile, shade, zero)
         r.small[5:6, :] += rows_sum(total)
+
+    def feed_back(item):
+        rows = rows_of(item)
         loaded("down", "slope")
 
         @pl.loop(0, units // 256)
@@ -1115,10 +1112,7 @@
             value = (dactive * r.slope[rows, lanes].astype(jnp.float32)).astype(low)
             r.dhidden[rows, lanes] = value
             summed = rows_sum(fold(value.astype(jnp.float32)))
-            if item == 0:
-                r.bias_sum[0:1, lanes] = summed
-            else:
-                r.bias_sum[0:1, lanes] += summed
+            r.bias_sum[item : item + 1, lanes] = summed
 
         loaded("up")
 
@@ -1244,8 +1238,9 @@
         for c in (0, 2):
             value = rows_sum(fold(r.dproject[c].astype(jnp.float32)))
             r.small[6:7, (c // 2) * local : (c // 2 + 1) * local] = value
-        r.small[7:8, :] = r.bias_sum[0:1, :width]
-        r.small[8:9, :] = r.bias_sum[0:1, width:]
+        total = rows_sum(r.bias_sum[0:items, :])
+        r.small[7:8, :] = total[:, :width]
+        r.small[8:9, :] = total[:, width:]
 
     def input_back(item):
         sent["pn%d" % item].wait_recv()
@@ -1281,6 +1276,7 @@
     tasks = {"kv": join_heads, "og": grad_out_weight, "bias": bias_sums}
     for index in range(2):
         for name, work in (
+            ("sh", shade_rows),
             ("ffn", feed_back),
             ("gd", grad_down),
             ("gu", grad_up),
@@ -1310,17 +1306,30 @@
         copy.wait_send()
 
 
+PATHS = {
+    "t": "yso",
+    "k": "yso",
+    "d0": "yso",
+    "d1": "yso",
+    "u0": "yso",
+    "u1": "yso",
+    "o": "yso",
+    "q2": "yso",
+    "q1": "yso",
+    "q0": "yso",
+}
+
 ORDER = (
-    "k.sA", "t.sA", "ffn0", "ffn1", "gd1", "d1.s0", "gu1", "u1.s0", "d1.s1", "t.sB", "gd0", "u1.s1",
-    "d0.s0", "gu0", "u0.s0", "d0.s1", "ln0", "u0.s1", "at0", "d1.s2", "k.sB", "t.s1", "ln1", "at1",
-    "d0.s2", "d1.s2b", "og", "o.s0", "u1.s2", "kv", "p0", "p1", "gq2", "q2.s0", "o.s1", "gq1",
-    "q1.s0", "q2.s1", "gq0", "q0.s0", "q1.s1", "d0.s2b", "d1.s3", "u0.s2", "q0.s1", "bias", "u1.s2b", "t.s2",
-    "d0.s3", "d1.s3b", "u0.s2b", "u1.s3", "f0", "o.s2", "k.s1", "t.s2b", "d0.s3b", "q2.s2", "d1.s4", "u0.s3",
-    "u1.s3b", "q1.s2", "f1", "t.s3", "o.s2b", "q0.s2", "d0.s4", "q2.s2b", "u0.s3b", "sm0", "o.s3", "t.s3b",
-    "k.s2", "q1.s2b", "u1.s4", "d1.s5", "q2.s3", "o.s3b", "sm1", "q0.s2b", "q1.s3", "q2.s3b", "k.s2b", "sm2",
-    "u0.s4", "q0.s3", "q1.s3b", "d0.s5", "t.s4", "k.s3", "sm3", "q0.s3b", "u1.s5", "o.s4", "d1.s6", "k.s3b",
-    "u0.s5", "sm4", "q2.s4", "d0.s6", "t.s5", "q1.s4", "u1.s6", "q0.s4", "o.s5", "u0.s6", "k.s4", "q2.s5",
-    "t.s6", "q1.s5", "o.s6", "q0.s5", "q2.s6", "k.s5", "q1.s6", "q0.s6", "k.s6",
+    "sh1", "sh0", "gd1", "d1.s0", "ffn0", "d1.s1", "k.sA", "gd0", "d0.s0", "ffn1", "gu0", "u0.s0",
+    "k.sB", "d0.s1", "gu1", "d1.s2", "u0.s1", "u1.s0", "t.sA", "ln0", "at0", "d1.s2b", "u1.s1", "t.sB",
+    "d0.s2", "ln1", "at1", "d1.s3", "og", "o.s0", "u0.s2", "d0.s2b", "kv", "bias", "o.s1", "gq0",
+    "p0", "k.s1", "d1.s3b", "p1", "u1.s2", "gq2", "u0.s2b", "gq1", "o.s2", "d0.s3", "q2.s0", "q0.s0",
+    "q1.s0", "d1.s4", "q2.s1", "q0.s1", "q1.s1", "t.s1", "k.s2", "u1.s2b", "u0.s3", "o.s2b", "d0.s3b", "d1.s5",
+    "f0", "d1.s6", "k.s2b", "u1.s3", "q2.s2", "u0.s3b", "o.s3", "q0.s2", "d0.s4", "q1.s2", "f1", "k.s3",
+    "sm0", "u1.s3b", "q2.s2b", "t.s2", "sm1", "u0.s4", "o.s3b", "q0.s2b", "d0.s5", "q1.s2b", "sm2", "k.s3b",
+    "d0.s6", "u1.s4", "q2.s3", "u0.s5", "t.s2b", "o.s4", "u0.s6", "q0.s3", "q1.s3", "sm3", "u1.s5", "k.s4",
+    "q2.s3b", "t.s3", "u1.s6", "sm4", "o.s5", "q0.s3b", "q1.s3b", "o.s6", "q2.s4", "t.s3b", "k.s5", "q0.s4",
+    "q1.s4", "k.s6", "q2.s5", "t.s4", "q2.s6", "q0.s5", "q0.s6", "q1.s5", "q1.s6", "t.s5", "t.s6",
 )
 
 LOADED = (

time: 232 us -> 211 us (0.909)
  Pallas kernels: 231 us -> 210 us
    pallas_call x1, Pallas kernels: 132 us -> 117 us  [backward_section(): pl.pallas_call(functools.partial(backward_kernel, tuple(layout)), out_sha...]
    pallas_call x1, Pallas kernels: 46.4 us -> 39.2 us  [forward_section(): pl.pallas_call(forward_kernel, out_shape=[jax.ShapeDtypeStruct(*one) for...]
where the time goes in v1:
time: 211 us
  Pallas kernels  210 us (100%)
    pallas_call x1, Pallas kernels, backward_section(): pl.pallas_call(functools.partial(backward_kernel, tuple(layout)), out_sha...  117 us
    pallas_call x1, Pallas kernels, decoder_section(): pl.pallas_call(decoder_kernel, out_shape=[jax.ShapeDtypeStruct((DEPTH, SI...  42.5 us
    pallas_call x1, Pallas kernels, forward_section(): pl.pallas_call(forward_kernel, out_shape=[jax.ShapeDtypeStruct(*one) for...  39.2 us
    pallas_call x1, Pallas kernels, finish_section(): pl.pallas_call(functools.partial(finish_kernel, count), out_shape=[jax.Sh...  11 us

profile of v1, /device:TPU:0, one launch (start us, length us, event | category | flops | bytes accessed | tf_op | source)
XLA Modules:
  0.0 210.9 jit_solution(8666352098992433444)
XLA Ops:
  0.6 39.2 %forward_section.1 = (bf16[512,768]{1,0:T(8,128)(2,1)}, bf16[512,384]{1,0:T(8,128)(2,1)}, bf16[2,2,512,384]{3,2,1,0:T(8,128)(2,1)}, bf16[2,6,512,256]{3,2,1,0:T(...) custom-call(bf16[2,256,768]{2,1,0:T(8,128)(2,1)} %refs_2_.1, ...), custom_call_target="tpu_custom_call" | custom-call | tf_op jit(solution)/shard_map/forward_section/pallas_call | solution.py:858
  39.9 42.5 %decoder_section.1 = (bf16[8,8,2,16,128]{4,3,2,1,0:T(8,128)(2,1)}, bf16[2,256,768]{2,1,0:T(8,128)(2,1)}, bf16[2,256,768]{2,1,0:T(8,128)(2,1)}, bf16[2,768,512]{2,1,0:T(8,128)(2,1)}, bf16[2,3584,128]{2,1,0:T(8,128)(2,1)}) custom-call(bf16[256,768]{1,0:T(8,128)(2,1)} %get-tuple-element.49.tapped, bf16[768,1024]{1,0:T(8,128)(2,1)} %tconv.1, ...), custom_call_target="tpu_custom_call" | custom-call | tf_op jit(solution)/shard_map/decoder_section/pallas_call | solution.py:448
  82.3 117.4 %backward_section.1 = (bf16[2,256,768]{2,1,0:T(8,128)(2,1)}, f32[16,768]{1,0:T(8,128)}, bf16[2,768,768]{2,1,0:T(8,128)(2,1)}, bf16[2,768,768]{2,1,0:T(8,128)(2,1...) custom-call(bf16[2,256,768]{2,1,0:T(8,128)(2,1)} %refs_0_.1, ...), custom_call_target="tpu_custom_call" | custom-call | tf_op jit(solution)/shard_map/backward_section/pallas_call | solution.py:1415
  199.7 11.0 %finish.1 = (f32[3,768,384]{2,1,0:T(8,128)}, f32[384,768]{1,0:T(8,128)}, f32[768,1536]{1,0:T(8,128)}, f32[2,768,768]{2,1,0:T(8,128)}, f32[768,512]{1,0:T(8,128)}...) custom-call(bf16[3,768,384]{2,1,0:T(8,128)(2,1)} %get-tuple-element., ...), custom_call_target="tpu_custom_call" | custom-call | tf_op jit(solution)/shard_map/finish/pallas_call | solution.py:581

commit v2 on v1

--- a/solution.py
+++ b/solution.py
@@ -198,15 +198,37 @@
 
 def decoder_kernel(
     tapped,
+    tconv_hbm,
+    kernels_hbm,
+    grad_decoded_hbm,
+    crop_shape,
+    grad_out_hbm,
+    down_hbm,
+    slope_hbm,
+    up_hbm,
+    decoded_hbm,
+    block_all_hbm,
+    dtap_all_hbm,
+    grad_tconv_hbm,
+    grad_kernels_hbm,
+    ddown_hbm,
+    dhidden_hbm,
+    two_hbm,
+    bias_sum,
+    shift_sum,
     tconv,
     kernels,
     grad_decoded,
-    crop_shape,
+    grad_out,
+    down,
+    slope,
+    up,
     decoded,
-    block_all,
-    dtap_all,
     grad_tconv,
     grad_kernels,
+    ddown,
+    dhidden,
+    two,
     mask,
     inverse,
     field_one,
@@ -228,15 +250,42 @@
     dtap_from,
     sums_mine,
     sums_from,
+    load_sem,
+    store_sem,
     send,
     recv,
 ):
     dp, blk, tensor, near, far, first = place()
     core, cross, beside, side, over = peers()
-    greet([core, cross])
     low = jnp.bfloat16
     row_tiles = ROWS // PAIR
-
+    slab, width = tapped.shape
+    units = dhidden.shape[1]
+    own_rows = rows_at(tensor * slab, slab)
+    loads = {}
+    for index, (name, src, dst) in enumerate(
+        (
+            ("tconv", tconv_hbm, tconv),
+            ("kernels", kernels_hbm, kernels),
+            ("grad_decoded", grad_decoded_hbm, grad_decoded),
+            ("grad_out", grad_out_hbm.at[tensor], grad_out),
+            ("down", down_hbm, down),
+            ("slope", slope_hbm.at[own_rows], slope),
+            ("up", up_hbm, up),
+        )
+    ):
+        copy = pltpu.make_async_copy(src, dst, load_sem.at[index])
+        copy.start()
+        loads[name] = copy
+
+    stores = []
+
+    def store(src, dst):
+        copy = pltpu.make_async_copy(src, dst, store_sem.at[len(stores)])
+        copy.start()
+        stores.append(copy)
+
+    store(tapped, block_all_hbm.at[tensor])
     copies = []
 
     def start(index, src, dst, device):
@@ -244,8 +293,6 @@
         copy.start()
         copies.append(copy)
         return copy
-
-    give_tapped = start(0, tapped, tapped_from, cross)
 
     depth_end, side_end = extents(crop_shape[tensor])
     row = lax.broadcasted_iota(jnp.int32, mask.shape, 0)
@@ -258,6 +305,11 @@
     voxels = (8 * depth_end * side_end * side_end).astype(jnp.float32)
     inverse[...] = 1.0 / jnp.full(inverse.shape, voxels)
 
+    for field in (field_one, field_two, dlevel_two, dlevel_one):
+        clear_rims(field, blk)
+    greet([core, cross])
+    give_tapped = start(0, tapped, tapped_from, cross)
+
     before, after = shift_matrix(-1), shift_matrix(1)
 
     def send_edge(index, field):
@@ -286,9 +338,8 @@
 
     zero_pair = (jnp.zeros((1, PAIR), jnp.float32), jnp.zeros((1, PAIR), jnp.float32))
 
-    for field in (field_one, field_two, dlevel_two, dlevel_one):
-        clear_rims(field, blk)
     weave = weave_matrix()
+    loads["tconv"].wait()
     for piece in range(2):
         tokens = slice(piece * CH, (piece + 1) * CH)
         for a in range(2):
@@ -310,6 +361,7 @@
         place_rows(field_one, before, after, step, level_one[rows_of(step), :].astype(low))
 
     edge = send_edge(1, field_one)
+    loads["kernels"].wait()
     lay_kernel(kernels, 0, weights_one)
     conv(field_one, weights_one, dot, level_one, edge.wait_recv)
 
@@ -348,6 +400,8 @@
     copy = totals(1, forward_sums(level_two))
     lay_flipped(kernels, 0, flipped_one)
     mean_two, scale_two = mean_and_scale(1, copy)
+
+    loads["grad_decoded"].wait()
 
     def two_depths(ref, step, b):
         return ref[pl.ds(2 * step, 2), :, b].reshape(PAIR, CH)
@@ -373,6 +427,8 @@
         )
 
     copy = totals(2, lax.fori_loop(0, row_tiles, decode, zero_pair))
+
+    store(decoded, decoded_hbm)
 
     def level_grad(slot, copy, level, scale, field, turned):
         mean_grad, mean_cross = means(slot, copy)
@@ -428,55 +484,120 @@
         for index in range(2):
             at = ((index + 1) * PADDED_TAPS - 1) * 64
             grad_kernels[half, at : at + 64, :] = jnp.zeros((64, CH), low)
+    store(grad_tconv, grad_tconv_hbm)
+
+    loads["grad_out"].wait()
+    tile = 64
+
+    def shade(step, total):
+        at = rows_at(step * tile, tile)
+        value = grad_out[at, :].astype(jnp.float32) + dtap_mine[at, :].astype(jnp.float32)
+        value = value.astype(low)
+        ddown[at, :] = value
+        return total + fold(value.astype(jnp.float32))
+
+    shift_sum[...] = lax.fori_loop(0, slab // tile, shade, jnp.zeros((8, width), jnp.float32))
+    store(ddown, ddown_hbm)
+    loads["down"].wait()
+    loads["slope"].wait()
+
+    @pl.loop(0, units // 256)
+    def _(step):
+        lanes = pl.ds(pl.multiple_of(step * 256, 256), 256)
+        dactive = nt_dot(ddown[...], down[lanes, :])
+        value = (dactive * slope[:, lanes].astype(jnp.float32)).astype(low)
+        dhidden[:, lanes] = value
+        bias_sum[:, lanes] = fold(value.astype(jnp.float32))
+
+    store(dhidden, dhidden_hbm)
+    loads["up"].wait()
+
+    @pl.loop(0, width // 256)
+    def _(step):
+        lanes = pl.ds(pl.multiple_of(step * 256, 256), 256)
+        two[:, lanes] = nt_dot(dhidden[...], up[lanes, :]).astype(low)
+
+    store(two, two_hbm)
     kernel_grad(field_two, turned_two, 1, grad_kernels, tensor)
     kernel_grad(field_one, turned_one, 0, grad_kernels, tensor)
+    store(grad_kernels, grad_kernels_hbm)
+    store(dtap_mine, dtap_all_hbm.at[tensor])
     give_tapped.wait_recv()
-    block_all[tensor] = tapped[...]
-    block_all[1 - tensor] = tapped_from[...]
+    store(tapped_from, block_all_hbm.at[1 - tensor])
     give_dtap.wait_recv()
-    dtap_all[tensor] = dtap_mine[...]
-    dtap_all[1 - tensor] = dtap_from[...]
+    store(dtap_from, dtap_all_hbm.at[1 - tensor])
     for copy in copies:
         copy.wait_send()
-
-
-def decoder_section(tapped, tconv_weight, kernels, grad_decoded, crop_shape):
+    for copy in stores:
+        copy.wait()
+
+
+def decoder_section(
+    tapped, tconv_weight, kernels, grad_decoded, crop_shape, grad_out, down, slope, up
+):
     low = jnp.bfloat16
+    wide = jnp.float32
+    slab, width = tapped.shape
+    units = down.shape[0]
     vmem = pl.BlockSpec(memory_space=pltpu.VMEM)
+    hbm = pl.BlockSpec(memory_space=pl.ANY)
     field = pltpu.VMEM((3, DEPTH + 2, SIDE + 2, WIDE, PAIR), low)
-    plane = pltpu.VMEM((ROWS, PAIR), jnp.float32)
-    return pl.pallas_call(
+    plane = pltpu.VMEM((ROWS, PAIR), wide)
+    kept = {
+        "decoded": (DEPTH, SIDE, 2, WIDE, CH),
+        "grad_tconv": (2, width, tconv_weight.shape[1] // 2),
+        "grad_kernels": (2, 2 * PADDED_TAPS * 64, CH),
+        "ddown": (slab, width),
+        "dhidden": (slab, units),
+        "two": (slab, width),
+    }
+    block = (2, slab, width)
+    shapes = [kept["decoded"], block, block] + list(kept.values())[1:]
+    names = ["decoded", "block_all", "dtap"] + list(kept)[1:] + ["bias_own", "shift_own"]
+    dma = pltpu.SemaphoreType.DMA
+    results = pl.pallas_call(
         decoder_kernel,
-        out_shape=[
-            jax.ShapeDtypeStruct((DEPTH, SIDE, 2, WIDE, CH), low),
-            jax.ShapeDtypeStruct((2,) + tapped.shape, low),
-            jax.ShapeDtypeStruct((2,) + tapped.shape, low),
-            jax.ShapeDtypeStruct((2, tapped.shape[1], tconv_weight.shape[1] // 2), low),
-            jax.ShapeDtypeStruct((2, PADDED_TAPS * CH, CH), low),
+        out_shape=[jax.ShapeDtypeStruct(shape, low) for shape in shapes]
+        + [
+            jax.ShapeDtypeStruct((8, units), wide),
+            jax.ShapeDtypeStruct((8, width), wide),
         ],
-        in_specs=[vmem] * 4 + [pl.BlockSpec(memory_space=pltpu.SMEM)],
-        out_specs=[vmem] * 5,
-        scratch_shapes=[pltpu.VMEM((ROWS, CH), jnp.float32), pltpu.VMEM((8, CH), jnp.float32)]
+        in_specs=[vmem] + [hbm] * 3 + [pl.BlockSpec(memory_space=pltpu.SMEM)] + [hbm] * 4,
+        out_specs=[hbm] * 8 + [vmem] * 2,
+        scratch_shapes=[
+            pltpu.VMEM(array.shape, array.dtype) for array in (tconv_weight, kernels, grad_decoded)
+        ]
+        + [
+            pltpu.VMEM((slab, width), low),
+            pltpu.VMEM(down.shape, low),
+            pltpu.VMEM((slab, units), low),
+            pltpu.VMEM(up.shape, low),
+        ]
+        + [pltpu.VMEM(shape, low) for shape in kept.values()]
+        + [pltpu.VMEM((ROWS, CH), wide), pltpu.VMEM((8, CH), wide)]
         + [field] * 4
         + [pltpu.VMEM((9, 4 * CH, PAIR), low)] * 2
         + [pltpu.VMEM((9, PAIR, 4 * CH), low)] * 2
         + [plane] * 3
         + [pltpu.VMEM((PAIR, ROWS), low)] * 2
         + [
-            pltpu.VMEM((tapped.shape[0], tconv_weight.shape[1]), low),
+            pltpu.VMEM((slab, tconv_weight.shape[1]), low),
             pltpu.VMEM(tapped.shape, low),
             pltpu.VMEM(tapped.shape, low),
             pltpu.VMEM(tapped.shape, low),
-            pltpu.VMEM((4, 8, CH), jnp.float32),
-            pltpu.VMEM((4, 8, CH), jnp.float32),
-            pltpu.SemaphoreType.DMA((10,)),
-            pltpu.SemaphoreType.DMA((10,)),
+            pltpu.VMEM((4, 8, CH), wide),
+            pltpu.VMEM((4, 8, CH), wide),
+            dma((7,)),
+            dma((10,)),
+            dma((10,)),
+            dma((10,)),
         ],
         name="decoder_section",
         compiler_params=pltpu.CompilerParams(
             collective_id=1, has_side_effects=True, vmem_limit_bytes=60 * 2**20
         ),
-    )(tapped, tconv_weight, kernels, grad_decoded, crop_shape)
+    )(tapped, tconv_weight, kernels, grad_decoded, crop_shape, grad_out, down, slope, up)
+    return dict(zip(names, results))
 
 
 def widen_rows(src, dst, tile=64):
@@ -535,8 +656,15 @@
         elif len(src.shape) == 3:
             for part in range(src.shape[0]):
                 widen_rows(low.at[part], wide.at[part])
-                columns = src.shape[2]
-                store(wide.at[part], dst.at[:, pl.ds(part * columns, columns)])
+                rows, columns = src.shape[1:]
+                across = dst.shape[1] // columns
+                store(
+                    wide.at[part],
+                    dst.at[
+                        pl.ds(part // across * rows, rows),
+                        pl.ds(part % across * columns, columns),
+                    ],
+                )
         elif len(dst.shape) == 2:
             widen_rows(low, wide)
             rows, columns = dst.shape[0], src.shape[1]
@@ -562,12 +690,12 @@
     wide = jnp.float32
     local = totals["qkv"].shape[2]
     width = totals["qkv"].shape[1]
-    units = totals["up"].shape[2] * 2
+    units = totals["up"].shape[2] * 4
     shapes = {
         "qkv": totals["qkv"].shape,
         "out": (local, width),
         "up": (width, units),
-        "down": totals["down"].shape,
+        "down": (units, width),
         "tconv": totals["tconv"].shape,
         "kernels": (2, 64, 27 * CH),
     }
@@ -593,7 +721,7 @@
         + [pltpu.VMEM(array.shape, array.dtype) for array in passed]
         + [
             pltpu.SemaphoreType.DMA((count,)),
-            pltpu.SemaphoreType.DMA((16,)),
+            pltpu.SemaphoreType.DMA((24,)),
             pltpu.SemaphoreType.DMA((3,)),
         ],
         name="finish",
@@ -1030,8 +1158,15 @@
     half_width = width // 2
 
     loads = {}
+    own_rows = rows_at(tensor * slab, slab)
+    landing = {
+        "two_own": r.two_mine.at[tensor],
+        "ddown_own": r.ddown.at[own_rows],
+        "dhidden_own": r.dhidden.at[own_rows],
+    }
     for index, name in enumerate(LOADED):
-        copy = pltpu.make_async_copy(getattr(r, name + "_hbm"), getattr(r, name), r.load_sem.at[index])
+        target = landing[name] if name in landing else getattr(r, name)
+        copy = pltpu.make_async_copy(getattr(r, name + "_hbm"), target, r.load_sem.at[index])
         copy.start()
         loads[name] = copy
     keep_full = {}
@@ -1055,7 +1190,7 @@
         return copy
 
     sums = {}
-    for h in range(2):
+    for h in range(4):
         sums["d%d" % h] = ("down%d" % h, r.own_down.at[h], r.total_down.at[h])
         sums["u%d" % h] = ("up%d" % h, r.own_up.at[h], r.total_up.at[h])
     sums["o"] = ("out", r.own_out, r.total_out)
@@ -1069,7 +1204,7 @@
     }
 
     def rows_of(item):
-        return slice(item * slab, (item + 1) * slab)
+        return rows_at(item * slab, slab)
 
     def lanes_of(step, size=256):
         return pl.ds(pl.multiple_of(step * size, size), size)
@@ -1092,16 +1227,24 @@
                 loads[name].wait()
                 waited.add(name)
 
-    def shade_rows(item):
+    own, other = tensor, 1 - tensor
+
+    def take_own():
+        loaded("two_own", "shift_own")
+        r.small[5:6, :] += rows_sum(r.shift_own[...])
+        sent["dn0"] = start(0, r.two_mine.at[own], r.two_from.at[own], cross)
+
+    def shade_other():
         def shade(step, total):
-            value = dout_rows(item, rows_at(step * tile, tile)).astype(low)
-            r.ddown[rows_at(item * slab + step * tile, tile), :] = value
+            value = dout_rows(other, rows_at(step * tile, tile)).astype(low)
+            r.ddown[rows_at(other * slab + step * tile, tile), :] = value
             return total + fold(value.astype(jnp.float32))
 
         total = lax.fori_loop(0, slab // tile, shade, zero)
         r.small[5:6, :] += rows_sum(total)
 
-    def feed_back(item):
+    def feed_back():
+        item = other
         rows = rows_of(item)
         loaded("down", "slope")
 
@@ -1112,7 +1255,7 @@
             value = (dactive * r.slope[rows, lanes].astype(jnp.float32)).astype(low)
             r.dhidden[rows, lanes] = value
             summed = rows_sum(fold(value.astype(jnp.float32)))
-            r.bias_sum[item : item + 1, lanes] = summed
+            r.bias_sum[0:1, lanes] = summed
 
         loaded("up")
 
@@ -1121,29 +1264,34 @@
             value = nt_dot(r.dhidden[rows, :], r.up[lanes_of(step), :])
             r.two_mine[item, :, lanes_of(step)] = value.astype(low)
 
-        sent["dn%d" % item] = start(item, r.two_mine.at[item], r.two_from.at[item], cross)
+        sent["dn1"] = start(1, r.two_mine.at[item], r.two_from.at[item], cross)
 
     def grad_down(h):
-        loaded("active")
+        loaded("active", "ddown_own")
 
         @pl.loop(0, units // 2 // 256)
         def _(step):
             lanes = pl.ds(pl.multiple_of(h * (units // 2) + step * 256, 256), 256)
-            r.own_down[h, lanes_of(step), :] = tn_dot(r.active[:, lanes], r.ddown[...]).astype(low)
+            value = tn_dot(r.active[:, lanes], r.ddown[...]).astype(low)
+            for part in range(2):
+                columns = slice(part * half_width, (part + 1) * half_width)
+                r.own_down[2 * h + part, lanes_of(step), :] = value[:, columns]
 
     def grad_up(h):
-        loaded("normed_two")
+        loaded("normed_two", "dhidden_own")
 
         @pl.loop(0, width // 256)
         def _(step):
             right = r.dhidden[:, h * (units // 2) : (h + 1) * (units // 2)]
-            r.own_up[h, lanes_of(step), :] = tn_dot(r.normed_two[:, lanes_of(step)], right).astype(
-                low
-            )
-
-    def middle_back(item):
+            value = tn_dot(r.normed_two[:, lanes_of(step)], right).astype(low)
+            for part in range(2):
+                columns = slice(part * (units // 4), (part + 1) * (units // 4))
+                r.own_up[2 * h + part, lanes_of(step), :] = value[:, columns]
+
+    def middle_back(index):
+        item = (other, own)[index]
         loaded("middle")
-        sent["dn%d" % item].wait_recv()
+        sent["dn%d" % index].wait_recv()
 
         def back(step, totals):
             at = rows_at(step * tile, tile)
@@ -1165,7 +1313,8 @@
         for row, total in zip((2, 3, 4), totals):
             r.small[row : row + 1, :] += rows_sum(total)
 
-    def attention_back(item):
+    def attention_back(index):
+        item = (other, own)[index]
         loaded("out_weight", "key_value", "query", "probs")
         rows = rows_of(item)
         r.keys_turned[...] = r.key_value[item, 0].astype(jnp.float32).T.astype(low)
@@ -1198,7 +1347,7 @@
             r.dproject[2, rows, lanes] = dvalues[:slab]
             r.give_kv[item, 0, :, lanes] = dkeys[slab:]
             r.give_kv[item, 1, :, lanes] = dvalues[slab:]
-        sent["kv%d" % item] = start(2 + item, r.give_kv.at[item], r.got_kv.at[item], core)
+        sent["kv%d" % index] = start(2 + index, r.give_kv.at[item], r.got_kv.at[item], core)
 
     def grad_out_weight():
         loaded("mixed")
@@ -1207,15 +1356,16 @@
             r.own_out[h * local : (h + 1) * local, :] = value.astype(low)
 
     def join_heads():
-        for item in range(items):
-            sent["kv%d" % item].wait_recv()
+        for index, item in enumerate((other, own)):
+            sent["kv%d" % index].wait_recv()
             rows = rows_of(item)
             for c in range(2):
                 value = r.dproject[1 + c, rows, :].astype(jnp.float32)
                 value = value + r.got_kv[item, c].astype(jnp.float32)
                 r.dproject[1 + c, rows, :] = value.astype(low)
 
-    def project_back(item):
+    def project_back(index):
+        item = (other, own)[index]
         loaded("qkv")
         rows = rows_of(item)
 
@@ -1228,7 +1378,7 @@
                 value = part if value is None else value + part
             r.one_mine[item, :, lanes] = value.astype(low)
 
-        sent["pn%d" % item] = start(4 + item, r.one_mine.at[item], r.one_from.at[item], cross)
+        sent["pn%d" % index] = start(4 + index, r.one_mine.at[item], r.one_from.at[item], cross)
 
     def grad_qkv(c):
         loaded("normed_one")
@@ -1238,12 +1388,15 @@
         for c in (0, 2):
             value = rows_sum(fold(r.dproject[c].astype(jnp.float32)))
             r.small[6:7, (c // 2) * local : (c // 2 + 1) * local] = value
-        total = rows_sum(r.bias_sum[0:items, :])
+        loaded("bias_own")
+        total = r.bias_sum[0:1, :] + rows_sum(r.bias_own[...])
         r.small[7:8, :] = total[:, :width]
         r.small[8:9, :] = total[:, width:]
 
-    def input_back(item):
-        sent["pn%d" % item].wait_recv()
+    def input_back(index):
+        item = (own, other)[index]
+        loaded("block_in")
+        sent["pn%d" % index].wait_recv()
 
         def back(step, totals):
             at = rows_at(step * tile, tile)
@@ -1273,11 +1426,17 @@
         else:
             r.small_total[...] = r.small_sum[4]
 
-    tasks = {"kv": join_heads, "og": grad_out_weight, "bias": bias_sums}
+    tasks = {
+        "sh0": take_own,
+        "sh1": shade_other,
+        "ffn0": lambda: None,
+        "ffn1": feed_back,
+        "kv": join_heads,
+        "og": grad_out_weight,
+        "bias": bias_sums,
+    }
     for index in range(2):
         for name, work in (
-            ("sh", shade_rows),
-            ("ffn", feed_back),
             ("gd", grad_down),
             ("gu", grad_up),
             ("ln", middle_back),
@@ -1307,36 +1466,48 @@
 
 
 PATHS = {
+    "d2": "yso",
+    "d3": "yso",
+    "u2": "yso",
+    "u3": "yso",
     "t": "yso",
     "k": "yso",
     "d0": "yso",
     "d1": "yso",
-    "u0": "yso",
+    "u0": "syo",
     "u1": "yso",
     "o": "yso",
-    "q2": "yso",
+    "q2": "syo",
     "q1": "yso",
     "q0": "yso",
 }
 
 ORDER = (
-    "sh1", "sh0", "gd1", "d1.s0", "ffn0", "d1.s1", "k.sA", "gd0", "d0.s0", "ffn1", "gu0", "u0.s0",
-    "k.sB", "d0.s1", "gu1", "d1.s2", "u0.s1", "u1.s0", "t.sA", "ln0", "at0", "d1.s2b", "u1.s1", "t.sB",
-    "d0.s2", "ln1", "at1", "d1.s3", "og", "o.s0", "u0.s2", "d0.s2b", "kv", "bias", "o.s1", "gq0",
-    "p0", "k.s1", "d1.s3b", "p1", "u1.s2", "gq2", "u0.s2b", "gq1", "o.s2", "d0.s3", "q2.s0", "q0.s0",
-    "q1.s0", "d1.s4", "q2.s1", "q0.s1", "q1.s1", "t.s1", "k.s2", "u1.s2b", "u0.s3", "o.s2b", "d0.s3b", "d1.s5",
-    "f0", "d1.s6", "k.s2b", "u1.s3", "q2.s2", "u0.s3b", "o.s3", "q0.s2", "d0.s4", "q1.s2", "f1", "k.s3",
-    "sm0", "u1.s3b", "q2.s2b", "t.s2", "sm1", "u0.s4", "o.s3b", "q0.s2b", "d0.s5", "q1.s2b", "sm2", "k.s3b",
-    "d0.s6", "u1.s4", "q2.s3", "u0.s5", "t.s2b", "o.s4", "u0.s6", "q0.s3", "q1.s3", "sm3", "u1.s5", "k.s4",
-    "q2.s3b", "t.s3", "u1.s6", "sm4", "o.s5", "q0.s3b", "q1.s3b", "o.s6", "q2.s4", "t.s3b", "k.s5", "q0.s4",
-    "q1.s4", "k.s6", "q2.s5", "t.s4", "q2.s6", "q0.s5", "q0.s6", "q1.s5", "q1.s6", "t.s5", "t.s6",
+    "k.sA", "sh0", "sh1", "gd0", "d1.s0", "gd1", "d2.s0", "k.sB", "d1.s1", "d3.s0", "d0.s0", "ffn0",
+    "ffn1", "d3.s1", "gu0", "u0.s0", "u1.s0", "d2.s1", "d0.s1", "d1.s2", "gu1", "u0.s1", "u2.s0", "ln0",
+    "u1.s1", "d3.s2", "d1.s2b", "u3.s0", "at0", "d2.s2", "u2.s1", "u3.s1", "u0.s2", "t.sA", "d3.s2b", "d0.s2",
+    "d1.s3", "k.s1", "d2.s2b", "t.sB", "u1.s2", "d3.s3", "d0.s2b", "d1.s3b", "u2.s2", "d2.s3", "u1.s2b", "d3.s3b",
+    "u3.s2", "ln1", "d0.s3", "d1.s4", "u0.s2b", "at1", "u1.s3", "og", "o.s0", "d3.s4", "d2.s3b", "u2.s2b",
+    "k.s2", "u3.s2b", "kv", "bias", "gq2", "t.s1", "d1.s5", "u0.s3", "gq0", "u1.s3b", "p0", "d2.s4",
+    "gq1", "d3.s5", "p1", "u2.s3", "q1.s0", "q0.s0", "d0.s3b", "k.s2b", "q2.s0", "d1.s6", "o.s1", "d3.s6",
+    "u3.s3", "q1.s1", "u0.s3b", "t.s2", "q0.s1", "q2.s1", "u1.s4", "u2.s3b", "d2.s5", "d0.s4", "k.s3", "d2.s6",
+    "f0", "o.s2", "t.s2b", "u3.s3b", "q1.s2", "q2.s2", "u0.s4", "u2.s4", "k.s3b", "f1", "sm0", "t.s3",
+    "o.s2b", "q0.s2", "u1.s5", "u3.s4", "sm1", "q1.s2b", "u1.s6", "d0.s5", "q2.s2b", "u0.s5", "d0.s6", "u0.s6",
+    "k.s4", "u2.s5", "t.s3b", "o.s3", "u2.s6", "q0.s2b", "u3.s5", "q1.s3", "sm2", "q2.s3", "u3.s6", "t.s4",
+    "o.s3b", "q0.s3", "k.s5", "q1.s3b", "sm3", "q2.s3b", "k.s6", "o.s4", "t.s5", "sm4", "q0.s3b", "q1.s4",
+    "q2.s4", "t.s6", "q0.s4", "o.s5", "o.s6", "q2.s5", "q1.s5", "q2.s6", "q1.s6", "q0.s5", "q0.s6",
 )
 
+LANDED = ("two_own", "ddown_own", "dhidden_own")
 LOADED = (
+    "two_own",
+    "shift_own",
+    "ddown_own",
+    "active",
     "down",
     "slope",
     "up",
-    "active",
+    "dhidden_own",
     "normed_two",
     "middle",
     "out_weight",
@@ -1346,6 +1517,8 @@
     "mixed",
     "qkv",
     "normed_one",
+    "block_in",
+    "bias_own",
 )
 
 
@@ -1358,17 +1531,21 @@
     units = arrays["down"].shape[0]
     patches = arrays["key_value"].shape[2]
     kernel_rows = arrays["grad_kernels"].shape[1]
-    near = ["grad_out", "dtap", "block_in", "gains"]
+    near = ["grad_out", "dtap", "gains"]
     distant = list(LOADED) + ["grad_kernels", "grad_tconv"]
     totals = {
-        "down": (2, units // 2, width),
-        "up": (2, width, units // 2),
+        "down": (4, units // 2, width // 2),
+        "up": (4, width, units // 4),
         "out": (2 * local, width // 2),
         "qkv": (3, width, local),
         "kernels": (kernel_rows, CH),
         "tconv": arrays["grad_tconv"].shape[1:],
     }
-    scratch = {name: pltpu.VMEM(arrays[name].shape, arrays[name].dtype) for name in LOADED}
+    scratch = {
+        name: pltpu.VMEM(arrays[name].shape, arrays[name].dtype)
+        for name in LOADED
+        if name not in LANDED
+    }
     for name, shape in totals.items():
         full = name in ("kernels", "tconv")
         rows, columns = shape[-2:]
@@ -1405,9 +1582,9 @@
     scratch["load_sem"] = dma((len(LOADED) + 2,))
     scratch["send"] = dma((10,))
     scratch["recv"] = dma((10,))
-    scratch["sum_send"] = dma((10, COPIES))
-    scratch["sum_recv"] = dma((10, COPIES))
-    scratch["sum_local"] = dma((10,))
+    scratch["sum_send"] = dma((14, COPIES))
+    scratch["sum_recv"] = dma((14, COPIES))
+    scratch["sum_local"] = dma((14,))
     outputs = ["grad_input", "small_total"] + ["total_" + name for name in totals]
     layout = near + [name + "_hbm" for name in distant] + outputs + list(scratch)
     vmem = pl.BlockSpec(memory_space=pltpu.VMEM)
@@ -1469,17 +1646,26 @@
         down_weight,
         crop_shape,
     )
-    decoded, block_all, dtap, grad_tconv, grad_kernels = decoder_section(
+    tap = decoder_section(
         tapped,
         tconv_weight,
         kernels,
         grad_decoded.reshape(DEPTH, SIDE, 2, WIDE, CH),
         crop_shape,
+        grad_out,
+        down_weight,
+        slope,
+        up_weight,
     )
     result = backward_section(
         {
             "grad_out": grad_out,
-            "dtap": dtap,
+            "dtap": tap["dtap"],
+            "two_own": tap["two"],
+            "shift_own": tap["shift_own"],
+            "ddown_own": tap["ddown"],
+            "dhidden_own": tap["dhidden"],
+            "bias_own": tap["bias_own"],
             "block_in": block_in,
             "gains": norm_gains,
             "down": down_weight,
@@ -1495,8 +1681,8 @@
             "mixed": mixed,
             "qkv": qkv_weight,
             "normed_one": normed_one,
-            "grad_kernels": grad_kernels,
-            "grad_tconv": grad_tconv,
+            "grad_kernels": tap["grad_kernels"],
+            "grad_tconv": tap["grad_tconv"],
         }
     )
     small = result["small_total"]
@@ -1509,7 +1695,7 @@
             name: lax.psum(array, "dp", axis_index_groups=same) for name, array in totals.items()
         }
     sums, passed, smalls = finish_section(
-        totals, (block_all, decoded, result["grad_input"]), small
+        totals, (tap["block_all"], tap["decoded"], result["grad_input"]), small
     )
     return (
         passed[0],
@@ -1522,7 +1708,7 @@
         sums["out"],
         sums["up"],
         smalls[3],
-        sums["down"].reshape(down_weight.shape),
+        sums["down"],
         sums["tconv"],
         sums["kernels"].transpose(0, 2, 1),
     )

time: 211 us -> 213 us (level); the launches traced: 211 us -> 209 us
  no operation moved by 1% of the time
where the time goes in v2:
time: 213 us; the launch traced here: 209 us
  Pallas kernels  208 us (98%)
    pallas_call x1, Pallas kernels, backward_section(): pl.pallas_call(functools.partial(backward_kernel, tuple(layout)), out_sha...  117 us
    pallas_call x1, Pallas kernels, decoder_section(): pl.pallas_call(decoder_kernel, out_shape=[jax.ShapeDtypeStruct(shape, low...  41.1 us
    pallas_call x1, Pallas kernels, forward_section(): pl.pallas_call(forward_kernel, out_shape=[jax.ShapeDtypeStruct(*one) for...  39.2 us
    pallas_call x1, Pallas kernels, finish_section(): pl.pallas_call(functools.partial(finish_kernel, count), out_shape=[jax.Sh...  11.1 us

profile of v2, /device:TPU:0, one launch (start us, length us, event | category | flops | bytes accessed | tf_op | source)
XLA Modules:
  0.0 208.9 jit_solution(4685986939919411027)
XLA Ops:
  0.6 39.2 %forward_section.1 = (bf16[512,768]{1,0:T(8,128)(2,1)}, bf16[512,384]{1,0:T(8,128)(2,1)}, bf16[2,2,512,384]{3,2,1,0:T(8,128)(2,1)}, bf16[2,6,512,256]{3,2,1,0:T(...) custom-call(bf16[2,256,768]{2,1,0:T(8,128)(2,1)} %refs_20_.1, ...), custom_call_target="tpu_custom_call" | custom-call | tf_op jit(solution)/shard_map/forward_section/pallas_call | solution.py:986
  39.9 41.1 %decoder_section.1 = (bf16[8,8,2,16,128]{4,3,2,1,0:T(8,128)(2,1)}, bf16[2,256,768]{2,1,0:T(8,128)(2,1)}, bf16[2,256,768]{2,1,0:T(8,128)(2,1)}, bf16[2,768,512]{2...) custom-call(bf16[256,768]{1,0:T(8,128)(2,1)} %get-tuple-element.54.t, ...), custom_call_target="tpu_custom_call" | custom-call | tf_op jit(solution)/shard_map/decoder_section/pallas_call | solution.py:558
  81.0 116.6 %backward_section.1 = (bf16[2,256,768]{2,1,0:T(8,128)(2,1)}, f32[16,768]{1,0:T(8,128)}, bf16[4,768,384]{2,1,0:T(8,128)(2,1)}, bf16[4,768,384]{2,1,0:T(8,128)(2,1...) custom-call(bf16[2,256,768]{2,1,0:T(8,128)(2,1)} %refs_0_.1, ...), custom_call_target="tpu_custom_call" | custom-call | tf_op jit(solution)/shard_map/backward_section/pallas_call | solution.py:1592
  197.7 11.1 %finish.1 = (f32[3,768,384]{2,1,0:T(8,128)}, f32[384,768]{1,0:T(8,128)}, f32[768,1536]{1,0:T(8,128)}, f32[1536,768]{1,0:T(8,128)}, f32[768,512]{1,0:T(8,128)}, /...) custom-call(bf16[3,768,384]{2,1,0:T(8,128)(2,1)} %get-tuple-element., ...), custom_call_target="tpu_custom_call" | custom-call | tf_op jit(solution)/shard_map/finish/pallas_call | solution.py:709
